TPU v7x, 32 devices: a whole 2x2x4 slice. The times are simulated.
32 devices in a mesh: seq: 8 (over y, x, core), tp: 4 (over z).
Axes of the slice: x: 2, y: 2, z: 4, core: 2. Of those that a mesh axis runs over, the one named last changes fastest.
Arguments:
- hidden_in: bfloat16 [4, 4096, 1024], P(None, 'seq'), may hold values from -6 to 6
- query_weight: bfloat16 [1024, 1024], P('seq', 'tp'), may hold values from -0.1875 to 0.1875
- key_weight: bfloat16 [1024, 1024], P('seq', 'tp'), may hold values from -0.1875 to 0.1875
- value_weight: bfloat16 [1024, 1024], P('seq', 'tp'), may hold values from -0.1875 to 0.1875
- gate_weight: bfloat16 [1024, 1024], P('seq', 'tp'), may hold values from -0.1875 to 0.1875
- out_weight: bfloat16 [1024, 1024], P('tp', 'seq'), may hold values from -0.1875 to 0.1875
- left_weight: bfloat16 [1024, 2816], P('seq', 'tp'), may hold values from -0.1875 to 0.1875
- right_weight: bfloat16 [1024, 2816], P('seq', 'tp'), may hold values from -0.1875 to 0.1875
- down_weight: bfloat16 [2816, 1024], P('tp', 'seq'), may hold values from -0.109375 to 0.109375
- decay_rate: float32 [8], P('tp'), may hold values from 0 to 1, as said below
- seq_bounds: int32 [4], replicated, may hold values from 1 to 4095, as said below
- out_cotangent: bfloat16 [4, 4096, 1024], P(None, 'seq'), may hold values from -6 to 6
Outputs:
- output: bfloat16 [4, 4096, 1024], P(None, 'seq')
- input_grad: float32 [4, 4096, 1024], P(None, 'seq')
- query_grad: float32 [1024, 1024], P('seq', 'tp')
- key_grad: float32 [1024, 1024], P('seq', 'tp')
- value_grad: float32 [1024, 1024], P('seq', 'tp')
- gate_grad: float32 [1024, 1024], P('seq', 'tp')
- out_grad: float32 [1024, 1024], P('tp', 'seq')
- left_grad: float32 [1024, 2816], P('seq', 'tp')
- right_grad: float32 [1024, 2816], P('seq', 'tp')
- down_grad: float32 [2816, 1024], P('tp', 'seq')
Inputs may be any that keep to these rules, and one draw needn't show every extreme that they name: Micro-batch m holds two sequences, rows below seq_bounds[m] and the rest; the boundary lies within the first or the last 512 rows of the micro-batch and never on a multiple of 512. A head's state shrinks by exp(-decay_rate) a row.
All inputs are finite; a program needn't handle non-finite values.
Results may differ from a plain program's by a relative error of at most 0.014.
Values may be sent and summed in bfloat16 or wider, within the bound.
A program may use at most 192 MiB of HBM per device.

v0:
```python
import math

import jax
import jax.numpy as jnp
from jax import lax
from jax.sharding import PartitionSpec as P

D = 1024
HEAD = 128


EPSILON = 1e-06
HIGHEST_PRECISION = lax.Precision.HIGHEST


def entering(value, axis, join, neutral, backward):
    count, mine = (lax.axis_size(axis), lax.axis_index(axis))
    pieces = jax.tree.map(lambda part: lax.all_gather(part, axis), value)
    if backward:
        pieces = jax.tree.map(lambda part: part[::-1], pieces)
        mine = count - 1 - mine
    subtotal = jax.tree.map(
        lambda part, zero: jnp.full_like(part, 0) + jnp.asarray(zero, part.dtype), value, neutral
    )

    def step(position, subtotal):
        longer = join(subtotal, jax.tree.map(lambda part: part[position], pieces))
        return jax.tree.map(lambda new, old: jnp.where(position < mine, new, old), longer, subtotal)

    return lax.fori_loop(0, count - 1, step, subtotal)


def swish_parts(pre_act):
    logistic = jax.nn.sigmoid(pre_act)
    return (pre_act * logistic, logistic * (1.0 + pre_act * (1.0 - logistic)))


def rotate(rows_in, cosine_table, sine_table, signed):
    halfway = rows_in.shape[-1] // 2
    front_half = rows_in[..., :halfway]
    back_half = rows_in[..., halfway:]
    return jnp.concatenate(
        [
            front_half * cosine_table - signed * back_half * sine_table,
            signed * front_half * sine_table + back_half * cosine_table,
        ],
        axis=-1,
    )


def combine_forward(earlier, following):
    return (earlier[0] * following[0], following[0][:, None, None] * earlier[1] + following[1])


def combine_backward(farther, nearer):
    return (farther[0] * nearer[0], nearer[1] + nearer[0][:, None, None] * farther[1])


def collect_weights(
    query_weight,
    key_weight,
    value_weight,
    gate_weight,
    out_weight,
    left_weight,
    right_weight,
    down_weight,
):
    return (
        lax.all_gather(query_weight, "seq", axis=0, tiled=True),
        lax.all_gather(key_weight, "seq", axis=0, tiled=True),
        lax.all_gather(value_weight, "seq", axis=0, tiled=True),
        lax.all_gather(gate_weight, "seq", axis=0, tiled=True),
        lax.all_gather(out_weight, "seq", axis=1, tiled=True),
        lax.all_gather(left_weight, "seq", axis=0, tiled=True),
        lax.all_gather(right_weight, "seq", axis=0, tiled=True),
        lax.all_gather(down_weight, "seq", axis=1, tiled=True),
    )


def state_prefix(factor, local_state):
    neutral = (jnp.ones_like(factor), jnp.zeros_like(local_state))
    return entering((factor, local_state), "seq", combine_forward, neutral, False)[1]


def state_suffix(factor, state_grad):
    neutral = (jnp.ones_like(factor), jnp.zeros_like(state_grad))
    return entering((factor, state_grad), "seq", combine_backward, neutral, True)[1]


def body(
    hidden_in,
    query_weight,
    key_weight,
    value_weight,
    gate_weight,
    out_weight,
    left_weight,
    right_weight,
    down_weight,
    decay_rate,
    seq_bounds,
    out_cotangent,
):
    row_count = hidden_in.shape[1]
    batch_count = hidden_in.shape[0]
    local_heads = decay_rate.shape[0]
    heads_shape = (row_count, local_heads, HEAD)
    device = lax.axis_index("seq")
    offsets = jnp.arange(row_count, dtype=jnp.int32)
    positions = device * row_count + offsets
    frequency = jnp.exp(
        jnp.arange(HEAD // 2, dtype=jnp.float32) * (-2.0 * math.log(10000.0) / HEAD)
    )
    angles = positions.astype(jnp.float32)[:, None] * frequency[None, :]
    cosine_table = jnp.cos(angles)[:, None, :]
    sine_table = jnp.sin(angles)[:, None, :]
    local_f = offsets.astype(jnp.float32)
    distance = local_f[:, None] - local_f[None, :]
    causal = distance >= 0.0
    distance_pos = jnp.maximum(distance, 0.0)
    accum = None
    outputs = []
    in_grads = []
    for batch_index in range(batch_count):
        gathered = collect_weights(
            query_weight,
            key_weight,
            value_weight,
            gate_weight,
            out_weight,
            left_weight,
            right_weight,
            down_weight,
        )
        query_full, key_full, value_full, gate_full, out_full, left_full, right_full, down_full = (
            gathered
        )
        boundary = seq_bounds[batch_index]
        segment = (positions >= boundary).astype(jnp.int32)
        before = (device * row_count - 1 >= boundary).astype(jnp.int32)
        last_segment = segment[row_count - 1]
        allowed = causal & (segment[:, None] == segment[None, :])
        decay = jnp.where(
            allowed[None], jnp.exp(-decay_rate[:, None, None] * distance_pos[None]), 0.0
        )
        coef_in = (
            jnp.exp(-decay_rate[None, :] * (local_f[:, None] + 1.0))
            * (segment == before).astype(jnp.float32)[:, None]
        )
        weight_loc = (
            jnp.exp(-decay_rate[None, :] * (row_count - 1.0 - local_f)[:, None])
            * (segment == last_segment).astype(jnp.float32)[:, None]
        )
        factor = jnp.where(last_segment == before, jnp.exp(-decay_rate * row_count), 0.0)
        input_rows = hidden_in[batch_index].astype(jnp.float32)
        inv_first = lax.rsqrt(jnp.mean(input_rows * input_rows, axis=-1, keepdims=True) + EPSILON)
        unit_first = input_rows * inv_first
        normed_first = unit_first.astype(jnp.bfloat16)
        query_pre = jnp.dot(normed_first, query_full, preferred_element_type=jnp.float32)
        key_pre = jnp.dot(normed_first, key_full, preferred_element_type=jnp.float32)
        value_pre = jnp.dot(normed_first, value_full, preferred_element_type=jnp.float32)
        gate_pre = jnp.dot(normed_first, gate_full, preferred_element_type=jnp.float32)
        query_act, query_slope = swish_parts(query_pre)
        key_act, key_slope = swish_parts(key_pre)
        query_rot = rotate(query_act.reshape(heads_shape), cosine_table, sine_table, 1.0).astype(
            jnp.bfloat16
        )
        key_rot = rotate(key_act.reshape(heads_shape), cosine_table, sine_table, 1.0).astype(
            jnp.bfloat16
        )
        value_rows = value_pre.astype(jnp.bfloat16).reshape(heads_shape)
        query_wide = query_rot.astype(jnp.float32)
        key_wide = key_rot.astype(jnp.float32)
        value_wide = value_rows.astype(jnp.float32)
        scores = jnp.einsum("ihe,jhe->hij", query_rot, key_rot, preferred_element_type=jnp.float32)
        attn_weights = (scores * decay).astype(jnp.bfloat16)
        inner_out = jnp.einsum(
            "hij,jhe->ihe", attn_weights, value_rows, preferred_element_type=jnp.float32
        )
        local_state = jnp.einsum(
            "jhe,jhf->hef",
            key_wide * weight_loc[:, :, None],
            value_wide,
            precision=HIGHEST_PRECISION,
        )
        incoming = state_prefix(factor, local_state)
        outer_out = coef_in[:, :, None] * jnp.einsum(
            "ihe,hef->ihf", query_wide, incoming, precision=HIGHEST_PRECISION
        )
        mixed_heads = (inner_out + outer_out).reshape(row_count, local_heads * HEAD)
        total_sq = lax.psum(jnp.sum(mixed_heads * mixed_heads, axis=-1), "tp")
        inv_mix = lax.rsqrt(total_sq / D + EPSILON)[:, None]
        unit_mix = mixed_heads * inv_mix
        gate_mix = (unit_mix * gate_pre).astype(jnp.bfloat16)
        attn_sum = lax.psum(jnp.dot(gate_mix, out_full, preferred_element_type=jnp.float32), "tp")
        resid_mid = input_rows + attn_sum
        inv_second = lax.rsqrt(jnp.mean(resid_mid * resid_mid, axis=-1, keepdims=True) + EPSILON)
        unit_second = resid_mid * inv_second
        normed_second = unit_second.astype(jnp.bfloat16)
        left_pre = jnp.dot(normed_second, left_full, preferred_element_type=jnp.float32)
        right_pre = jnp.dot(normed_second, right_full, preferred_element_type=jnp.float32)
        glu_product = (left_pre * right_pre).astype(jnp.bfloat16)
        glu_out = lax.psum(
            jnp.dot(glu_product, down_full, preferred_element_type=jnp.float32), "tp"
        )
        outputs.append((resid_mid + glu_out).astype(jnp.bfloat16))
        glu_cot = out_cotangent[batch_index]
        product_grad = jnp.einsum(
            "cd,fd->cf", glu_cot, down_full, preferred_element_type=jnp.float32
        )
        left_back = (product_grad * right_pre).astype(jnp.bfloat16)
        right_back = (product_grad * left_pre).astype(jnp.bfloat16)
        second_part = jnp.einsum(
            "cf,df->cd", left_back, left_full, preferred_element_type=jnp.float32
        ) + jnp.einsum("cf,df->cd", right_back, right_full, preferred_element_type=jnp.float32)
        second_back = lax.psum(second_part, "tp")
        mid_grad = glu_cot.astype(jnp.float32) + inv_second * (
            second_back - unit_second * jnp.mean(second_back * unit_second, axis=-1, keepdims=True)
        )
        attn_cot = mid_grad.astype(jnp.bfloat16)
        gate_mix_grad = jnp.einsum(
            "cd,kd->ck", attn_cot, out_full, preferred_element_type=jnp.float32
        )
        gate_back = (gate_mix_grad * unit_mix).astype(jnp.bfloat16)
        unit_mix_grad = gate_mix_grad * gate_pre
        mix_dot = lax.psum(jnp.sum(unit_mix_grad * unit_mix, axis=-1), "tp")
        heads_grad = (
            (inv_mix * (unit_mix_grad - unit_mix * (mix_dot / D)[:, None]))
            .astype(jnp.bfloat16)
            .reshape(heads_shape)
        )
        pair_grad = jnp.einsum(
            "ihe,jhe->hij", heads_grad, value_rows, preferred_element_type=jnp.float32
        ).astype(jnp.bfloat16)
        score_grad = pair_grad.astype(jnp.float32) * decay
        query_inner = jnp.einsum("hij,jhe->ihe", score_grad, key_wide, precision=HIGHEST_PRECISION)
        key_inner = jnp.einsum("hij,ihe->jhe", score_grad, query_wide, precision=HIGHEST_PRECISION)
        value_inner = jnp.einsum(
            "hij,ihe->jhe", attn_weights, heads_grad, preferred_element_type=jnp.float32
        )
        scaled_grad = heads_grad.astype(jnp.float32) * coef_in[:, :, None]
        query_outer = jnp.einsum("ihf,hef->ihe", scaled_grad, incoming, precision=HIGHEST_PRECISION)
        state_grad = jnp.einsum(
            "ihe,ihf->hef", query_wide, scaled_grad, precision=HIGHEST_PRECISION
        )
        later_grad = state_suffix(factor, state_grad)
        key_state = weight_loc[:, :, None] * jnp.einsum(
            "jhf,hef->jhe", value_wide, later_grad, precision=HIGHEST_PRECISION
        )
        value_state = weight_loc[:, :, None] * jnp.einsum(
            "jhe,hef->jhf", key_wide, later_grad, precision=HIGHEST_PRECISION
        )
        query_back = (
            rotate(query_inner + query_outer, cosine_table, sine_table, -1.0).reshape(row_count, -1)
            * query_slope
        ).astype(jnp.bfloat16)
        key_back = (
            rotate(key_inner + key_state, cosine_table, sine_table, -1.0).reshape(row_count, -1)
            * key_slope
        ).astype(jnp.bfloat16)
        value_back = (value_inner + value_state).reshape(row_count, -1).astype(jnp.bfloat16)
        fresh = (
            jnp.einsum("cd,ck->dk", normed_first, query_back, preferred_element_type=jnp.float32),
            jnp.einsum("cd,ck->dk", normed_first, key_back, preferred_element_type=jnp.float32),
            jnp.einsum("cd,ck->dk", normed_first, value_back, preferred_element_type=jnp.float32),
            jnp.einsum("cd,ck->dk", normed_first, gate_back, preferred_element_type=jnp.float32),
            jnp.einsum("ck,cd->kd", gate_mix, attn_cot, preferred_element_type=jnp.float32),
            jnp.einsum("cd,cf->df", normed_second, left_back, preferred_element_type=jnp.float32),
            jnp.einsum("cd,cf->df", normed_second, right_back, preferred_element_type=jnp.float32),
            jnp.einsum("cf,cd->fd", glu_product, glu_cot, preferred_element_type=jnp.float32),
        )
        if accum is None:
            accum = list(fresh)
        else:
            accum = [older + newer for older, newer in zip(accum, fresh)]
        total = jnp.einsum("ck,dk->cd", query_back, query_full, preferred_element_type=jnp.float32)
        total = total + jnp.einsum(
            "ck,dk->cd", key_back, key_full, preferred_element_type=jnp.float32
        )
        total = total + jnp.einsum(
            "ck,dk->cd", value_back, value_full, preferred_element_type=jnp.float32
        )
        first_back = lax.psum(
            total
            + jnp.einsum("ck,dk->cd", gate_back, gate_full, preferred_element_type=jnp.float32),
            "tp",
        )
        input_back = mid_grad + inv_first * (
            first_back - unit_first * jnp.mean(first_back * unit_first, axis=-1, keepdims=True)
        )
        in_grads.append(input_back)
    summed = (
        lax.psum_scatter(accum[0], "seq", scatter_dimension=0, tiled=True),
        lax.psum_scatter(accum[1], "seq", scatter_dimension=0, tiled=True),
        lax.psum_scatter(accum[2], "seq", scatter_dimension=0, tiled=True),
        lax.psum_scatter(accum[3], "seq", scatter_dimension=0, tiled=True),
        lax.psum_scatter(accum[4], "seq", scatter_dimension=1, tiled=True),
        lax.psum_scatter(accum[5], "seq", scatter_dimension=0, tiled=True),
        lax.psum_scatter(accum[6], "seq", scatter_dimension=0, tiled=True),
        lax.psum_scatter(accum[7], "seq", scatter_dimension=1, tiled=True),
    )
    return (
        jnp.stack(outputs),
        jnp.stack(in_grads),
        summed[0],
        summed[1],
        summed[2],
        summed[3],
        summed[4],
        summed[5],
        summed[6],
        summed[7],
    )


def solution(mesh):
    return jax.shard_map(
        body,
        mesh=mesh,
        in_specs=(
            P(None, "seq", None),
            P("seq", "tp"),
            P("seq", "tp"),
            P("seq", "tp"),
            P("seq", "tp"),
            P("tp", "seq"),
            P("seq", "tp"),
            P("seq", "tp"),
            P("tp", "seq"),
            P("tp"),
            P(),
            P(None, "seq", None),
        ),
        out_specs=(
            P(None, "seq", None),
            P(None, "seq", None),
            P("seq", "tp"),
            P("seq", "tp"),
            P("seq", "tp"),
            P("seq", "tp"),
            P("tp", "seq"),
            P("seq", "tp"),
            P("seq", "tp"),
            P("tp", "seq"),
        ),
        check_vma=False,
    )
```

profile of v0, /device:TPU:0, one launch (start us, length us, event | category | flops | bytes accessed | tf_op | source)
XLA Modules:
  0.0 2147.2 jit_solution(13425586296212149464)
XLA Ops:
  18.8 11.6 all_gather.129
  34.4 9.5 all_gather.130
  53.2 9.2 all_gather.128
  77.4 13.8 all-reduce.4
  91.3 10.3 all_gather.135
  101.6 9.2 all_gather.136
  116.2 7.2 while.112
  127.4 12.0 psum.168
  145.9 81.9 %all-reduce.15.cloned.1.call-done = f32[512,1024]{1,0:T(8,128)} async-done(((f32[512,1024]{1,0:T(8,128)}), f32[512,1024]{1,0:T(8,128)}) %all-reduce.15.cloned.1.call-update) | async-done | bytes 2097168 | tf_op jit(solution)/shard_map/psum | solution.py:196
  227.9 4.5 multiply_reduce_fusion.7
  260.8 4.5 subtract_convert_fusion.1
  271.0 3.8 fusion.138
  296.4 3.7 fusion.330
  300.1 8.6 all-gather.24.cloned.1.call-done
  308.8 4.5 multiply_convert_fusion.19
  317.5 17.2 all-gather.36.cloned.1.call-done
  334.8 20.2 while.115
  355.0 6.0 all-gather.34.cloned.1.call-done
  360.9 20.2 while.114
  381.2 6.0 all-gather.32.cloned.1.call-done
  387.1 15.4 while.113
  411.4 11.9 all-reduce.6
  436.5 289.0 %all-reduce.21.cloned.1.call-done = (f32[512,1024]{1,0:T(8,128)}, f32[512,1024]{1,0:T(8,128)}, f32[512,1024]{1,0:T(8,128)}, f32[512,1024]{1,0:T(8,128)}) async-done(((f32[512,1024]{1,0:T(8,128)}, f32[512,1024]{1,0:T(8,128)}, f32[512,1024]{1,0:T(8,128)}, f32[512,1024]{1,0:T(8,128)}), (f32[512,1024]{1,0:T(8,128)}, f32[512,1024]{1,0:T(8,128)}, f32[512,1024]{1,0:T(8,128)}, ...) | async-done | bytes 8388624 | tf_op jit(solution)/shard_map/psum | solution.py:217
  725.5 5.5 multiply_reduce_fusion.3
  733.8 3.7 multiply_add_fusion.3
  739.0 9.6 psum.181
  786.7 15.5 while.116
  819.1 3.5 add_add_fusion.6
  825.1 3.5 fusion.331
  835.8 278.5 %all-reduce.19.cloned.1.call-done = (f32[512,1024]{1,0:T(8,128)}, f32[512,1024]{1,0:T(8,128)}, f32[512,1024]{1,0:T(8,128)}, f32[512,1024]{1,0:T(8,128)}) async-done(((f32[512,1024]{1,0:T(8,128)}, f32[512,1024]{1,0:T(8,128)}, f32[512,1024]{1,0:T(8,128)}, f32[512,1024]{1,0:T(8,128)}), (f32[512,1024]{1,0:T(8,128)}, f32[512,1024]{1,0:T(8,128)}, f32[512,1024]{1,0:T(8,128)}, ...) | async-done | bytes 8388624 | tf_op jit(solution)/shard_map/psum | solution.py:217
  1114.4 7.4 fusion.32
  1134.1 10.3 all-reduce.5
  1185.9 16.6 while.117
  1210.6 16.5 while.118
  1235.0 12.2 while.119
  1359.6 436.1 %all-reduce.17.cloned.1.call-done = (f32[512,1024]{1,0:T(8,128)}, f32[512,1024]{1,0:T(8,128)}, f32[512,1024]{1,0:T(8,128)}, f32[512,1024]{1,0:T(8,128)}, f32[512...) async-done(((f32[512,1024]{1,0:T(8,128)}, f32[512,1024]{1,0:T(8,128)}, f32[512,1024]{1,0:T(8,128)}, f32[512,1024]{1,0:T(8,128)}, f32[512,1024]{1,0:T(8,128)}, ...) | async-done | bytes 14680080 | tf_op jit(solution)/shard_map/psum | solution.py:204
  1795.7 4.4 fusion.39
  1802.0 5.5 fusion.43
  1810.2 6.8 fusion.36
  1817.0 5.1 pad_maximum_fusion
  1824.4 19.2 reduce-scatter.23.cloned.1.call-done
  1843.7 48.7 %reduce-scatter.21.cloned.1.call-done = f32[128,704]{0,1:T(8,128)} async-done(((f32[1024,704]{0,1:T(8,128)}), f32[128,704]{0,1:T(8,128)}) %reduce-scatter.21.cloned.1.call-update) | async-done | bytes 360464 | tf_op jit(solution)/shard_map/reduce_scatter | solution.py:300
  1892.4 49.1 %reduce-scatter.19.cloned.1.call-done = f32[128,704]{0,1:T(8,128)} async-done(((f32[1024,704]{0,1:T(8,128)}), f32[128,704]{0,1:T(8,128)}) %reduce-scatter.19.cloned.1.call-update) | async-done | bytes 360464 | tf_op jit(solution)/shard_map/reduce_scatter | solution.py:299
  1941.5 39.8 %reduce-scatter.17.cloned.1.call-done = f32[256,128]{1,0:T(8,128)} async-done(((f32[256,1024]{1,0:T(8,128)}), f32[256,128]{1,0:T(8,128)}) %reduce-scatter.17.cloned.1.call-update) | async-done | bytes 131088 | tf_op jit(solution)/shard_map/reduce_scatter | solution.py:298
  1981.3 39.6 %reduce-scatter.15.cloned.1.call-done = f32[128,256]{1,0:T(8,128)} async-done(((f32[1024,256]{1,0:T(8,128)}), f32[128,256]{1,0:T(8,128)}) %reduce-scatter.15.cloned.1.call-update) | async-done | bytes 131088 | tf_op jit(solution)/shard_map/reduce_scatter | solution.py:297
  2020.9 39.8 %reduce-scatter.13.cloned.1.call-done = f32[128,256]{1,0:T(8,128)} async-done(((f32[1024,256]{1,0:T(8,128)}), f32[128,256]{1,0:T(8,128)}) %reduce-scatter.13.cloned.1.call-update) | async-done | bytes 131088 | tf_op jit(solution)/shard_map/reduce_scatter | solution.py:296
  2060.7 39.8 %reduce-scatter.11.cloned.1.call-done = f32[128,256]{1,0:T(8,128)} async-done(((f32[1024,256]{1,0:T(8,128)}), f32[128,256]{1,0:T(8,128)}) %reduce-scatter.11.cloned.1.call-update) | async-done | bytes 131088 | tf_op jit(solution)/shard_map/reduce_scatter | solution.py:295
  2100.5 39.8 %reduce-scatter.9.cloned.1.call-done = f32[128,256]{1,0:T(8,128)} async-done(((f32[1024,256]{1,0:T(8,128)}), f32[128,256]{1,0:T(8,128)}) %reduce-scatter.9.cloned.1.call-update) | async-done | bytes 131088 | tf_op jit(solution)/shard_map/reduce_scatter | solution.py:294
  (1028 shorter events, 509.6 us)
Async XLA Ops:
  7.2 109.0 %all-gather.30.cloned.1.call-start = ((), (), s32[]{:S(2)}) async-start(), calls=%async_computation.20 | async-start | bytes 1179648 | tf_op jit(solution)/shard_map/all_gather | solution.py:18
  10.7 40.7 %copy-start.264 = (s32[512]{0:T(512)}, s32[512]{0:T(512)S(1)}, u32[]{:S(2)}) copy-start(s32[512]{0:T(512)S(1)} %get-tuple-element.1203) | copy-start | bytes 6148
  18.8 43.7 %copy-start.266 = (f32[512]{0:T(512)}, f32[512]{0:T(512)S(1)}, u32[]{:S(2)}) copy-start(f32[512]{0:T(512)S(1)} %add_rsqrt_fusion.11) | copy-start | bytes 6148
  30.4 219.3 %copy-start.33 = (bf16[1024,256]{1,0:T(8,128)(2,1)}, bf16[1024,256]{1,0:T(8,128)(2,1)S(1)}, u32[]{:S(2)}) copy-start(bf16[1024,256]{1,0:T(8,128)(2,1)S(1)} %all_gather.129) | copy-start | bytes 1572868
  43.9 210.4 %copy-start.36 = (bf16[1024,256]{1,0:T(8,128)(2,1)}, bf16[1024,256]{1,0:T(8,128)(2,1)S(1)}, u32[]{:S(2)}) copy-start(bf16[1024,256]{1,0:T(8,128)(2,1)S(1)} %all_gather.130) | copy-start | bytes 1572868
  62.4 221.7 %copy-start.39 = (bf16[1024,256]{1,0:T(8,128)(2,1)}, bf16[1024,256]{1,0:T(8,128)(2,1)S(1)}, u32[]{:S(2)}) copy-start(bf16[1024,256]{1,0:T(8,128)(2,1)S(1)} %all_gather.128) | copy-start | bytes 1572868
  64.4 60.5 %copy-start.114 = (bf16[512,256]{0,1:T(8,128)(2,1)}, bf16[512,256]{0,1:T(8,128)(2,1)S(1)}, u32[]{:S(2)}) copy-start(bf16[512,256]{0,1:T(8,128)(2,1)S(1)} %convolution_convert_fusion.7) | copy-start | bytes 786436
  66.2 25.0 %copy-start.248 = (bf16[128,256]{1,0:T(8,128)(2,1)S(1)}, bf16[128,256]{1,0:T(8,128)(2,1)}, u32[]{:S(2)}) copy-start(bf16[128,256]{1,0:T(8,128)(2,1)} %param.32) | copy-start | bytes 196612
  66.2 35.4 %copy-start.249 = (bf16[256,128]{1,0:T(8,128)(2,1)S(1)}, bf16[256,128]{1,0:T(8,128)(2,1)}, u32[]{:S(2)}) copy-start(bf16[256,128]{1,0:T(8,128)(2,1)} %param.33) | copy-start | bytes 196612
  68.8 22.4 %copy-start.126 = (bf16[512,2,128]{2,0,1:T(8,128)(2,1)}, bf16[512,2,128]{2,0,1:T(8,128)(2,1)S(1)}, u32[]{:S(2)}) copy-start(bf16[512,2,128]{2,0,1:T(8,128)(2,1)S(1)} %pad_maximum_fusion.11) | copy-start | bytes 786436
  69.4 42.7 %copy-start.263 = (s32[512]{0:T(512)S(1)}, s32[512]{0:T(512)}, u32[]{:S(2)}) copy-start(s32[512]{0:T(512)} %copy-done.262) | copy-start | bytes 6148
  69.4 42.7 %copy-start.265 = (s32[512]{0:T(512)S(1)}, s32[512]{0:T(512)}, u32[]{:S(2)}) copy-start(s32[512]{0:T(512)} %copy-done.264) | copy-start | bytes 6148
  72.9 40.9 %copy-start.277 = (f32[2]{0:T(128)}, f32[2]{0:T(128)S(1)}, u32[]{:S(2)}) copy-start(f32[2]{0:T(128)S(1)} %get-tuple-element.1162) | copy-start | bytes 28
  73.6 49.9 %copy-start.244 = (f32[512,2]{0,1:T(2,128)}, f32[512,2]{0,1:T(2,128)S(1)}, u32[]{:S(2)}) copy-start(f32[512,2]{0,1:T(2,128)S(1)} %get-tuple-element.1149) | copy-start | bytes 12292
  75.1 152.8 %all-reduce.15.cloned.1.call-start = ((), (), s32[]{:S(2)}) async-start(), calls=%async_computation.8 | async-start | bytes 4194304 | tf_op jit(solution)/shard_map/psum | solution.py:196
  123.4 18.7 copy-start.83
  144.0 126.9 %all-gather.28.cloned.1.call-start = ((), (), s32[]{:S(2)}) async-start(), calls=%async_computation.11 | async-start | bytes 1622016 | tf_op jit(solution)/shard_map/all_gather | solution.py:77
  144.7 151.7 %all-gather.26.cloned.1.call-start = ((), (), s32[]{:S(2)}) async-start(), calls=%async_computation.10 | async-start | bytes 1622016 | tf_op jit(solution)/shard_map/all_gather | solution.py:76
  145.3 163.4 %all-gather.24.cloned.1.call-start = ((), (), s32[]{:S(2)}) async-start(), calls=%async_computation.9 | async-start | bytes 1622016 | tf_op jit(solution)/shard_map/all_gather | solution.py:75
  145.9 188.9 %all-gather.36.cloned.1.call-start = ((), (), s32[]{:S(2)}) async-start(), calls=%async_computation.23 | async-start | bytes 1179648 | tf_op jit(solution)/shard_map/all_gather | solution.py:18
  232.4 198.9 %copy-start.227 = (f32[512]{0:T(512)}, f32[512]{0:T(512)S(1)}, u32[]{:S(2)}) copy-start(f32[512]{0:T(512)S(1)} %add_rsqrt_fusion.8) | copy-start | bytes 6148
  235.3 192.8 %copy-start.229 = (f32[512]{0:T(512)}, f32[512]{0:T(512)S(1)}, u32[]{:S(2)}) copy-start(f32[512]{0:T(512)S(1)} %add_rsqrt_fusion.5) | copy-start | bytes 6148
  249.7 173.6 %copy-start.231 = (f32[512]{0:T(512)}, f32[512]{0:T(512)S(1)}, u32[]{:S(2)}) copy-start(f32[512]{0:T(512)S(1)} %add_rsqrt_fusion.2) | copy-start | bytes 6148
  265.5 22.0 %copy-start.125 = (bf16[512,2,128]{2,0,1:T(8,128)(2,1)}, bf16[512,2,128]{2,0,1:T(8,128)(2,1)S(1)}, u32[]{:S(2)}) copy-start(bf16[512,2,128]{2,0,1:T(8,128)(2,1)S(1)} %pad_maximum_fusion.17) | copy-start | bytes 786436
  268.8 92.1 %all-gather.34.cloned.1.call-start = ((), (), s32[]{:S(2)}) async-start(), calls=%async_computation.22 | async-start | bytes 1179648 | tf_op jit(solution)/shard_map/all_gather | solution.py:18
  279.4 107.7 %all-gather.32.cloned.1.call-start = ((), (), s32[]{:S(2)}) async-start(), calls=%async_computation.21 | async-start | bytes 1179648 | tf_op jit(solution)/shard_map/all_gather | solution.py:18
  293.9 431.6 %all-reduce.21.cloned.1.call-start = ((), (), s32[]{:S(2)}) async-start(), calls=%async_computation.30 | async-start | bytes 16777216 | tf_op jit(solution)/shard_map/psum | solution.py:217
  435.2 290.3 %copy-start.250 = (f32[512]{0:T(512)S(1)}, f32[512]{0:T(512)}, u32[]{:S(2)}) copy-start(f32[512]{0:T(512)} %add_rsqrt_fusion.9) | copy-start | bytes 6148
  435.2 349.0 %all-gather.38.cloned.1.call-start = ((), (), s32[]{:S(2)}) async-start(), calls=%async_computation.24 | async-start | bytes 1179648 | tf_op jit(solution)/shard_map/all_gather | solution.py:18
  757.1 357.3 %all-reduce.19.cloned.1.call-start = ((), (), s32[]{:S(2)}) async-start(), calls=%async_computation.29 | async-start | bytes 16777216 | tf_op jit(solution)/shard_map/psum | solution.py:217
  784.2 19.2 copy-start.116
  784.2 19.2 copy-start.216
  822.6 360.9 %all-gather.40.cloned.1.call-start = ((), (), s32[]{:S(2)}) async-start(), calls=%async_computation.25 | async-start | bytes 1179648 | tf_op jit(solution)/shard_map/all_gather | solution.py:18
  833.3 281.0 %copy-start.12 = (f32[512,1024]{1,0:T(8,128)S(1)}, f32[512,1024]{1,0:T(8,128)}, u32[]{:S(2)}) copy-start(f32[512,1024]{1,0:T(8,128)} %get-tuple-element.1031) | copy-start | bytes 6291460
  833.3 281.0 %copy-start.252 = (f32[512]{0:T(512)S(1)}, f32[512]{0:T(512)}, u32[]{:S(2)}) copy-start(f32[512]{0:T(512)} %copy-done.251) | copy-start | bytes 6148
  1147.9 60.3 %all-gather.42.cloned.1.call-start = ((), (), s32[]{:S(2)}) async-start(), calls=%async_computation.26 | async-start | bytes 1179648 | tf_op jit(solution)/shard_map/all_gather | solution.py:18
  1164.2 68.6 %all-gather.44.cloned.1.call-start = ((), (), s32[]{:S(2)}) async-start(), calls=%async_computation.27 | async-start | bytes 1179648 | tf_op jit(solution)/shard_map/all_gather | solution.py:18
  1183.5 612.2 %all-reduce.17.cloned.1.call-start = ((), (), s32[]{:S(2)}) async-start(), calls=%async_computation.28 | async-start | bytes 29360128 | tf_op jit(solution)/shard_map/psum | solution.py:204
  1183.5 19.0 copy-start.236
  1208.3 18.8 copy-start.234
  1299.0 544.6 %reduce-scatter.23.cloned.1.call-start = ((), (), s32[]{:S(2)}) async-start(), calls=%async_computation.19 | async-start | bytes 3244032 | tf_op jit(solution)/shard_map/reduce_scatter | solution.py:301
  1307.8 584.5 %reduce-scatter.21.cloned.1.call-start = ((), (), s32[]{:S(2)}) async-start(), calls=%async_computation.18 | async-start | bytes 3244032 | tf_op jit(solution)/shard_map/reduce_scatter | solution.py:300
  1316.7 624.8 %reduce-scatter.19.cloned.1.call-start = ((), (), s32[]{:S(2)}) async-start(), calls=%async_computation.17 | async-start | bytes 3244032 | tf_op jit(solution)/shard_map/reduce_scatter | solution.py:299
  1324.5 656.8 %reduce-scatter.17.cloned.1.call-start = ((), (), s32[]{:S(2)}) async-start(), calls=%async_computation.16 | async-start | bytes 1179648 | tf_op jit(solution)/shard_map/reduce_scatter | solution.py:298
  1332.4 688.5 %reduce-scatter.15.cloned.1.call-start = ((), (), s32[]{:S(2)}) async-start(), calls=%async_computation.15 | async-start | bytes 1179648 | tf_op jit(solution)/shard_map/reduce_scatter | solution.py:297
  1339.3 721.4 %reduce-scatter.13.cloned.1.call-start = ((), (), s32[]{:S(2)}) async-start(), calls=%async_computation.14 | async-start | bytes 1179648 | tf_op jit(solution)/shard_map/reduce_scatter | solution.py:296
  1345.9 754.5 %reduce-scatter.11.cloned.1.call-start = ((), (), s32[]{:S(2)}) async-start(), calls=%async_computation.13 | async-start | bytes 1179648 | tf_op jit(solution)/shard_map/reduce_scatter | solution.py:295
  1352.6 787.7 %reduce-scatter.9.cloned.1.call-start = ((), (), s32[]{:S(2)}) async-start(), calls=%async_computation.12 | async-start | bytes 1179648 | tf_op jit(solution)/shard_map/reduce_scatter | solution.py:294
  (264 other events, 1040.9 us)
Sparse Core Ops, SparseCore 0:
  75.2 24.8 all-gather.29
  144.1 83.7 all-reduce.14
  229.9 24.2 all-gather.27
  256.1 25.3 all-gather.25
  283.4 25.3 all-gather.23
  311.2 23.4 all-gather.35
  337.4 23.5 all-gather.33
  363.6 23.5 all-gather.31
  435.3 290.1 all-reduce.20
  757.2 22.0 all-gather.37
  822.8 291.5 all-reduce.18
  1148.1 22.0 all-gather.39
  1172.2 23.5 all-gather.41
  1198.2 23.4 all-gather.43
  1299.2 496.5 all-reduce.16
  1799.9 43.7 reduce-scatter.22
  1847.5 44.8 reduce-scatter.20
  1896.6 44.8 reduce-scatter.18
  1945.2 35.9 reduce-scatter.16
  1984.9 35.9 reduce-scatter.14
  2024.6 35.9 reduce-scatter.12
  2064.4 35.9 reduce-scatter.10
  2104.2 35.9 reduce-scatter.8
where the time goes:
time: 2160 us; the launch traced here: 2150 us
  waiting for transfers between devices  1440 us (67%)
  matrix products  251 us (12%)
  other arithmetic  181 us (8%)
  local copies, waits for them, and re-layouts  139 us (6%)
  blocking collectives  107 us (5%)
  between operations  23.5 us (1%)
    psum x2, waiting for transfers between devices, body(): second_back = lax.psum(second_part, 'tp')  568 us
    psum x1, waiting for transfers between devices, body(): lax.psum(jnp.dot(glu_product, down_full, preferred_element_type=jnp.float...  436 us
    psum x1, waiting for transfers between devices, body(): lax.psum(jnp.dot(gate_mix, out_full, preferred_element_type=jnp.float32),...  81.9 us
    select_n x56, other arithmetic, step(): jnp.where(position < mine, new, old)  75.2 us
    unnamed x599, local copies, waits for them, and re-layouts  50.4 us
    reduce_scatter x1, waiting for transfers between devices, body(): lax.psum_scatter(accum[5], 'seq', scatter_dimension=0, tiled=True)  49.1 us
    reduce_scatter x1, waiting for transfers between devices, body(): lax.psum_scatter(accum[6], 'seq', scatter_dimension=0, tiled=True)  48.7 us
  transfers between devices with their start and end apart: 23, of which 16 were waited for; matrix products, arithmetic and copies ran while one was open for 15% of the time, Pallas kernels for 0%

commit v1 on v0

--- a/solution.py
+++ b/solution.py
@@ -1,8 +1,11 @@
+import functools
 import math
 
 import jax
 import jax.numpy as jnp
 from jax import lax
+from jax.experimental import pallas as pl
+from jax.experimental.pallas import tpu as pltpu
 from jax.sharding import PartitionSpec as P
 
 D = 1024
@@ -11,6 +14,458 @@
 
 EPSILON = 1e-06
 HIGHEST_PRECISION = lax.Precision.HIGHEST
+MESH = pl.DeviceIdType.MESH
+BF16 = jnp.bfloat16
+F32 = jnp.float32
+
+SEQ = 8
+TP = 4
+STRIPE = 128
+
+
+def place():
+    s, t = lax.axis_index("seq"), lax.axis_index("tp")
+    core = s % 2
+    column = (s // 2) % 2
+    line = s // 4
+    other = s + 1 - 2 * core
+    across_x = s + 2 * (1 - 2 * column)
+    across_y = s + 4 * (1 - 2 * line)
+    first = across_x + core * (across_y - across_x)
+    second = across_y + core * (across_x - across_y)
+    diagonal = across_x + across_y - s
+    return s, t, other, first, second, diagonal
+
+
+def nearest(t, step):
+    flip = t // 2
+    low = t + flip * (3 - 2 * t)
+    swap = low * (1 - step // 2)
+    index = step + swap * (1 - 2 * step)
+    return index + flip * (3 - 2 * index)
+
+
+def stripe(index):
+    return pl.ds(pl.multiple_of(index * STRIPE, STRIPE), STRIPE)
+
+
+def greet(devices):
+    barrier = pltpu.get_barrier_semaphore()
+    for device in devices:
+        pl.semaphore_signal(barrier, inc=1, device_id=device, device_id_type=MESH)
+
+
+def greet_line(t, s, here):
+    barrier = pltpu.get_barrier_semaphore()
+
+    @pl.when(t > 0)
+    def _():
+        pl.semaphore_signal(barrier, inc=1, device_id=(s, t - 1), device_id_type=MESH)
+
+    @pl.when(t < TP - 1)
+    def _():
+        pl.semaphore_signal(barrier, inc=1, device_id=(s, t + 1), device_id_type=MESH)
+
+    for device in here:
+        pl.semaphore_signal(barrier, inc=1, device_id=(device, t), device_id_type=MESH)
+    inner = jnp.where((t > 0) & (t < TP - 1), 1, 0)
+    pl.semaphore_wait(barrier, len(here) + 1 + inner)
+
+
+SENDS = ("first", "second", "other", "relay", "relay_other", "third_other", "fourth_other")
+
+
+def gather_kernel(count, *refs):
+    ins, outs = refs[:count], refs[count : 2 * count]
+    local_sem, up_sem, down_sem, line_sem, send_sem, first_sem, second_sem, other_sem = refs[2 * count :]
+    s, t, other, first, second, diagonal = place()
+    other_first = first + (second - s) + (other - s) - (first - s)
+    other_second = second + (first - s) + (other - s) - (second - s)
+    other_diagonal = diagonal + other - s
+    greet_line(t, s, (other, first, second))
+
+    def remote(src, w, owner, column, send, receive, device):
+        return pltpu.make_async_remote_copy(
+            src_ref=src,
+            dst_ref=outs[w].at[owner, :, stripe(column)],
+            send_sem=send,
+            recv_sem=receive,
+            device_id=device,
+            device_id_type=MESH,
+        )
+
+    def spot(w, owner, column):
+        return outs[w].at[owner, :, stripe(column)]
+
+    waits = []
+    items = [(w, step) for w in range(count) for step in range(TP)]
+
+    def own(w):
+        return pltpu.make_async_copy(ins[w], spot(w, t, s), local_sem.at[w])
+
+    def line_copies(w, owner, src):
+        up = remote(src, w, owner, s, up_sem.at[w, owner], line_sem.at[w, owner], (s, t + 1))
+        down = remote(src, w, owner, s, down_sem.at[w, owner], line_sem.at[w, owner], (s, t - 1))
+        return up, down
+
+    def plane_copies(index, w, owner, src):
+        return (
+            remote(src, w, owner, s, send_sem.at[index, 0], first_sem.at[index], (first, t)),
+            remote(src, w, owner, s, send_sem.at[index, 1], second_sem.at[index, 0], (second, t)),
+            remote(src, w, owner, s, send_sem.at[index, 2], other_sem.at[index, 0], (other, t)),
+        )
+
+    def relay_copies(index, w, owner):
+        src = spot(w, owner, first)
+        return (
+            remote(src, w, owner, first, send_sem.at[index, 3], second_sem.at[index, 1], (second, t)),
+            remote(src, w, owner, first, send_sem.at[index, 4], other_sem.at[index, 1], (other, t)),
+        )
+
+    def last_copies(index, w, owner):
+        return (
+            remote(spot(w, owner, second), w, owner, second, send_sem.at[index, 5], other_sem.at[index, 2], (other, t)),
+            remote(spot(w, owner, diagonal), w, owner, diagonal, send_sem.at[index, 6], other_sem.at[index, 3], (other, t)),
+        )
+
+    for index in range(len(items) + 2):
+        if index < len(items):
+            w, step = items[index]
+            owner = nearest(t, step)
+            if step == 0:
+                own(w).start()
+                src = ins[w]
+                up, down = line_copies(w, owner, src)
+                pl.when(t < TP - 1)(up.start)
+                pl.when(t > 0)(down.start)
+            else:
+                src = spot(w, owner, s)
+                up, down = line_copies(w, owner, src)
+                up.wait_recv()
+                pl.when((owner < t) & (t < TP - 1))(up.start)
+                pl.when((owner > t) & (t > 0))(down.start)
+            for copy in plane_copies(index, w, owner, src):
+                copy.start()
+        if 1 <= index <= len(items):
+            w, step = items[index - 1]
+            owner = nearest(t, step)
+            remote(spot(w, owner, first), w, owner, first, send_sem.at[index - 1, 0], first_sem.at[index - 1], (first, t)).wait_recv()
+            for copy in relay_copies(index - 1, w, owner):
+                copy.start()
+        if index >= 2:
+            w, step = items[index - 2]
+            owner = nearest(t, step)
+            for part, column in enumerate((second, diagonal)):
+                remote(spot(w, owner, column), w, owner, column, send_sem.at[index - 2, 1], second_sem.at[index - 2, part], (second, t)).wait_recv()
+            for copy in last_copies(index - 2, w, owner):
+                copy.start()
+    for index, (w, step) in enumerate(items):
+        owner = nearest(t, step)
+        for part, column in enumerate((other, other_first, other_second, other_diagonal)):
+            remote(spot(w, owner, column), w, owner, column, send_sem.at[index, 2], other_sem.at[index, part], (other, t)).wait_recv()
+        src = ins[w] if step == 0 else spot(w, owner, s)
+        up, down = line_copies(w, owner, src)
+        if step == 0:
+            own(w).wait()
+            pl.when(t < TP - 1)(up.wait_send)
+            pl.when(t > 0)(down.wait_send)
+        else:
+            pl.when((owner < t) & (t < TP - 1))(up.wait_send)
+            pl.when((owner > t) & (t > 0))(down.wait_send)
+        for copy in plane_copies(index, w, owner, src) + relay_copies(index, w, owner) + last_copies(index, w, owner):
+            copy.wait_send()
+
+
+def gather_weights(shards):
+    count = len(shards)
+    items = count * TP
+    dma = pltpu.SemaphoreType.DMA
+    return pl.pallas_call(
+        functools.partial(gather_kernel, count),
+        out_shape=[jax.ShapeDtypeStruct((TP, shard.shape[0], D), BF16) for shard in shards],
+        in_specs=[pl.BlockSpec(memory_space=pl.ANY)] * count,
+        out_specs=[pl.BlockSpec(memory_space=pl.ANY)] * count,
+        scratch_shapes=[
+            dma((count,)),
+            dma((count, TP)),
+            dma((count, TP)),
+            dma((count, TP)),
+            dma((items, 7)),
+            dma((items,)),
+            dma((items, 2)),
+            dma((items, 4)),
+        ],
+        compiler_params=pltpu.CompilerParams(collective_id=0, has_side_effects=True),
+        name="gather_weights",
+    )(*shards)
+
+
+ROWS_STEP = 64
+PIECES = 4
+
+
+def add_rows(target, *terms):
+    rows = target.shape[0]
+
+    @pl.loop(0, rows // ROWS_STEP)
+    def _(block):
+        part = pl.ds(pl.multiple_of(block * ROWS_STEP, ROWS_STEP), ROWS_STEP)
+        total = terms[0][part, :].astype(F32)
+        for term in terms[1:]:
+            total = total + term[part, :].astype(F32)
+        target[part, :] = total.astype(target.dtype)
+
+
+def reduce_kernel(count, spread, *refs):
+    grads, refs = refs[:count], refs[count:]
+    shares, refs = refs[:spread], refs[spread:]
+    outs, refs = refs[:count], refs[count:]
+    wholes, refs = refs[:spread], refs[spread:]
+    own, refs = refs[0], refs[1:]
+    other_land, refs = refs[:count], refs[count:]
+    second_land, refs = refs[:count], refs[count:]
+    first_land, refs = refs[:count], refs[count:]
+    below_land, refs = refs[:count], refs[count:]
+    above_land, refs = refs[:count], refs[count:]
+    (own_sem, other_send, other_recv, second_send, second_recv, first_send, first_recv,
+     line_send, below_recv, above_recv, share_local, share_up, share_down, share_recv) = refs
+    s, t, other, first, second, diagonal = place()
+    core = s % 2
+    greet_line(t, s, (other, first, second))
+
+    def remote(src, dst, send, receive, device):
+        return pltpu.make_async_remote_copy(
+            src_ref=src, dst_ref=dst, send_sem=send, recv_sem=receive, device_id=device, device_id_type=MESH
+        )
+
+    piece_rows = shares[0].shape[0] // PIECES
+    pieces = [(a, p) for p in range(PIECES) for a in range(spread)]
+
+    def piece(a, owner, p):
+        return wholes[a].at[owner, pl.ds(p * piece_rows, piece_rows), :]
+
+    def share_copies(a, p, owner, src):
+        sem = (a, p, owner)
+        return (
+            remote(src, piece(a, owner, p), share_up.at[sem], share_recv.at[sem], (s, t + 1)),
+            remote(src, piece(a, owner, p), share_down.at[sem], share_recv.at[sem], (s, t - 1)),
+        )
+
+    def own_piece(a, p):
+        return shares[a].at[pl.ds(p * piece_rows, piece_rows), :]
+
+    for a, p in pieces:
+        up, down = share_copies(a, p, t, own_piece(a, p))
+        pl.when(t < TP - 1)(up.start)
+        pl.when(t > 0)(down.start)
+        pltpu.make_async_copy(own_piece(a, p), piece(a, t, p), share_local.at[a, p]).start()
+
+    relays = [(a, p, step) for a, p in pieces for step in range(1, TP)]
+
+    def relay(index):
+        a, p, step = relays[index]
+        owner = nearest(t, step)
+        up, down = share_copies(a, p, owner, piece(a, owner, p))
+        up.wait_recv()
+        pl.when((owner < t) & (t < TP - 1))(up.start)
+        pl.when((owner > t) & (t > 0))(down.start)
+
+    items = [(w, step) for w in range(count) for step in reversed(range(TP))]
+    slots = own.shape[0]
+
+    def sends(index, w, owner):
+        return [
+            remote(
+                grads[w].at[owner, :, stripe(2 * chip + 1 - core)],
+                other_land[w].at[owner, chip],
+                other_send.at[index, chip],
+                other_recv.at[index, chip],
+                (other, t),
+            )
+            for chip in range(4)
+        ]
+
+    def loads(index, w, owner):
+        rows = grads[w].shape[1]
+        return [
+            pltpu.make_async_copy(
+                grads[w].at[owner, :, stripe(2 * chip + core)],
+                own.at[index % slots, chip, pl.ds(0, rows), :],
+                own_sem.at[index % slots, chip],
+            )
+            for chip in range(4)
+        ]
+
+    def to_second(index, w, owner):
+        return [
+            remote(
+                other_land[w].at[owner, column // 2],
+                second_land[w].at[owner, part],
+                second_send.at[index, part],
+                second_recv.at[index, part],
+                (second, t),
+            )
+            for part, column in enumerate((diagonal, second))
+        ]
+
+    def to_first(index, w, owner):
+        return remote(
+            second_land[w].at[owner, 0], first_land[w].at[owner], first_send.at[index], first_recv.at[index], (first, t)
+        )
+
+    def along(index, w, owner):
+        up = remote(
+            first_land[w].at[owner], below_land[w].at[owner], line_send.at[index], below_recv.at[w, owner], (s, t + 1)
+        )
+        down = remote(
+            first_land[w].at[owner], above_land[w].at[owner], line_send.at[index], above_recv.at[w, owner], (s, t - 1)
+        )
+        return up, down
+
+    total = len(items)
+    for tick in range(total + 4):
+        index = tick
+        if index < total:
+            w, step = items[index]
+            owner = nearest(t, step)
+            for copy in sends(index, w, owner) + loads(index, w, owner):
+                copy.start()
+        index = tick - 1
+        if 0 <= index < total:
+            w, step = items[index]
+            owner = nearest(t, step)
+            rows = grads[w].shape[1]
+            for copy in loads(index, w, owner):
+                copy.wait()
+            for copy in sends(index, w, owner):
+                copy.wait_recv()
+            for chip in range(4):
+                add_rows(
+                    other_land[w].at[owner, chip],
+                    other_land[w].at[owner, chip],
+                    own.at[index % slots, chip, pl.ds(0, rows), :],
+                )
+            for copy in to_second(index, w, owner):
+                copy.start()
+        index = tick - 2
+        if 0 <= index < total:
+            w, step = items[index]
+            owner = nearest(t, step)
+            for copy in to_second(index, w, owner):
+                copy.wait_recv()
+            add_rows(second_land[w].at[owner, 0], second_land[w].at[owner, 0], other_land[w].at[owner, first // 2])
+            to_first(index, w, owner).start()
+        index = tick - 3
+        if 0 <= index < total:
+            w, step = items[index]
+            owner = nearest(t, step)
+            to_first(index, w, owner).wait_recv()
+            add_rows(
+                first_land[w].at[owner],
+                first_land[w].at[owner],
+                other_land[w].at[owner, s // 2],
+                second_land[w].at[owner, 1],
+            )
+        index = tick - 4
+        if 0 <= index < total:
+            w, step = items[index]
+            owner = nearest(t, step)
+            up, down = along(index, w, owner)
+            if step:
+
+                @pl.when((owner > t) & (t > 0))
+                def _():
+                    up.wait_recv()
+                    add_rows(first_land[w].at[owner], first_land[w].at[owner], below_land[w].at[owner])
+
+                @pl.when((owner < t) & (t < TP - 1))
+                def _():
+                    down.wait_recv()
+                    add_rows(first_land[w].at[owner], first_land[w].at[owner], above_land[w].at[owner])
+
+                pl.when(owner > t)(up.start)
+                pl.when(owner < t)(down.start)
+            else:
+
+                @pl.when(t == 0)
+                def _():
+                    down.wait_recv()
+                    add_rows(outs[w], first_land[w].at[owner], above_land[w].at[owner])
+
+                @pl.when(t == TP - 1)
+                def _():
+                    up.wait_recv()
+                    add_rows(outs[w], first_land[w].at[owner], below_land[w].at[owner])
+
+                @pl.when((t > 0) & (t < TP - 1))
+                def _():
+                    up.wait_recv()
+                    down.wait_recv()
+                    add_rows(outs[w], first_land[w].at[owner], below_land[w].at[owner], above_land[w].at[owner])
+
+        if tick < len(relays):
+            relay(tick)
+
+    for index, (w, step) in enumerate(items):
+        owner = nearest(t, step)
+        for copy in sends(index, w, owner) + to_second(index, w, owner):
+            copy.wait_send()
+        to_first(index, w, owner).wait_send()
+        if step:
+            along(index, w, owner)[0].wait_send()
+    for a, p in pieces:
+        up, down = share_copies(a, p, t, own_piece(a, p))
+        pl.when(t < TP - 1)(up.wait_send)
+        pl.when(t > 0)(down.wait_send)
+        pltpu.make_async_copy(own_piece(a, p), piece(a, t, p), share_local.at[a, p]).wait()
+    for a, p, step in relays:
+        owner = nearest(t, step)
+        up, down = share_copies(a, p, owner, piece(a, owner, p))
+        pl.when((owner < t) & (t < TP - 1))(up.wait_send)
+        pl.when((owner > t) & (t > 0))(down.wait_send)
+
+
+def reduce_gradients(grads, shares):
+    count, spread = len(grads), len(shares)
+    items = count * TP
+    dma = pltpu.SemaphoreType.DMA
+    rows = [grad.shape[1] for grad in grads]
+    vmem = pl.BlockSpec(memory_space=pltpu.VMEM)
+    anywhere = pl.BlockSpec(memory_space=pl.ANY)
+    results = pl.pallas_call(
+        functools.partial(reduce_kernel, count, spread),
+        out_shape=[jax.ShapeDtypeStruct((r, STRIPE), F32) for r in rows]
+        + [jax.ShapeDtypeStruct((TP, *share.shape), share.dtype) for share in shares],
+        in_specs=[anywhere] * (count + spread),
+        out_specs=[vmem] * count + [anywhere] * spread,
+        scratch_shapes=[pltpu.VMEM((3, 4, max(rows), STRIPE), BF16)]
+        + [pltpu.VMEM((TP, 4, r, STRIPE), BF16) for r in rows]
+        + [pltpu.VMEM((TP, 2, r, STRIPE), BF16) for r in rows]
+        + [pltpu.VMEM((TP, r, STRIPE), BF16) for r in rows]
+        + [pltpu.VMEM((TP, r, STRIPE), BF16) for r in rows]
+        + [pltpu.VMEM((TP, r, STRIPE), BF16) for r in rows]
+        + [
+            dma((3, 4)),
+            dma((items, 4)),
+            dma((items, 4)),
+            dma((items, 2)),
+            dma((items, 2)),
+            dma((items,)),
+            dma((items,)),
+            dma((items,)),
+            dma((count, TP)),
+            dma((count, TP)),
+            dma((spread, PIECES)),
+            dma((spread, PIECES, TP)),
+            dma((spread, PIECES, TP)),
+            dma((spread, PIECES, TP)),
+        ],
+        compiler_params=pltpu.CompilerParams(
+            collective_id=1, has_side_effects=True, vmem_limit_bytes=56 * 2**20
+        ),
+        name="reduce_gradients",
+    )(*grads, *shares)
+    return results[:count], results[count:]
 
 
 def entering(value, axis, join, neutral, backward):
@@ -314,9 +769,196 @@
     )
 
 
+def dots(left, right, dims):
+    return lax.dot_general(left, right, (dims, ((), ())), preferred_element_type=F32)
+
+
+NN = ((1,), (0,))
+NT = ((1,), (1,))
+TN = ((0,), (0,))
+
+
+def fused_body(
+    hidden_in,
+    query_weight,
+    key_weight,
+    value_weight,
+    gate_weight,
+    out_weight,
+    left_weight,
+    right_weight,
+    down_weight,
+    decay_rate,
+    seq_bounds,
+    out_cotangent,
+):
+    row_count = hidden_in.shape[1]
+    device, batch = lax.axis_index("seq"), lax.axis_index("tp")
+    rates = lax.all_gather(decay_rate, "tp", axis=0, tiled=True)
+    heads = rates.shape[0]
+    shards = [
+        query_weight.T,
+        key_weight.T,
+        value_weight.T,
+        gate_weight.T,
+        out_weight,
+        left_weight.T,
+        right_weight.T,
+        down_weight,
+    ]
+    query_full, key_full, value_full, gate_full, out_full, left_full, right_full, down_full = [
+        whole.reshape(-1, D) for whole in gather_weights(shards)
+    ]
+    heads_shape = (row_count, heads, HEAD)
+    offsets = jnp.arange(row_count, dtype=jnp.int32)
+    positions = device * row_count + offsets
+    frequency = jnp.exp(
+        jnp.arange(HEAD // 2, dtype=F32) * (-2.0 * math.log(10000.0) / HEAD)
+    )
+    angles = positions.astype(F32)[:, None] * frequency[None, :]
+    cosine_table = jnp.cos(angles)[:, None, :]
+    sine_table = jnp.sin(angles)[:, None, :]
+    local_f = offsets.astype(F32)
+    distance = local_f[:, None] - local_f[None, :]
+    boundary = lax.dynamic_index_in_dim(seq_bounds, batch, 0, keepdims=False)
+    segment = (positions >= boundary).astype(jnp.int32)
+    before = (device * row_count - 1 >= boundary).astype(jnp.int32)
+    last_segment = segment[row_count - 1]
+    allowed = (distance >= 0.0) & (segment[:, None] == segment[None, :])
+    decay = jnp.where(allowed[None], jnp.exp(-rates[:, None, None] * jnp.maximum(distance, 0.0)[None]), 0.0)
+    coef_in = (
+        jnp.exp(-rates[None, :] * (local_f[:, None] + 1.0)) * (segment == before).astype(F32)[:, None]
+    )
+    weight_loc = (
+        jnp.exp(-rates[None, :] * (row_count - 1.0 - local_f)[:, None])
+        * (segment == last_segment).astype(F32)[:, None]
+    )
+    blocks = jnp.arange(SEQ)
+    ends = ((blocks + 1) * row_count - 1 >= boundary).astype(jnp.int32)
+    gap = (device - 1 - blocks).astype(F32)
+    prefix_coef = jnp.where(
+        ((blocks < device) & (ends == before))[:, None],
+        jnp.exp(-rates[None, :] * row_count * jnp.maximum(gap, 0.0)[:, None]),
+        0.0,
+    )
+    later_before = (blocks * row_count - 1 >= boundary).astype(jnp.int32)
+    later_gap = (blocks - 1 - device).astype(F32)
+    suffix_coef = jnp.where(
+        ((blocks > device) & (later_before == last_segment))[:, None],
+        jnp.exp(-rates[None, :] * row_count * jnp.maximum(later_gap, 0.0)[:, None]),
+        0.0,
+    )
+
+    def states(local, coef):
+        every = lax.all_gather(local.astype(BF16), "seq").astype(F32)
+        return jnp.sum(coef[:, :, None, None] * every, axis=0)
+
+    input_rows = lax.dynamic_index_in_dim(hidden_in, batch, 0, keepdims=False).astype(F32)
+    glu_cot = lax.dynamic_index_in_dim(out_cotangent, batch, 0, keepdims=False)
+    inv_first = lax.rsqrt(jnp.mean(input_rows * input_rows, axis=-1, keepdims=True) + EPSILON)
+    unit_first = input_rows * inv_first
+    normed_first = unit_first.astype(BF16)
+    query_pre = dots(normed_first, query_full, NT)
+    key_pre = dots(normed_first, key_full, NT)
+    value_pre = dots(normed_first, value_full, NT)
+    gate_pre = dots(normed_first, gate_full, NT)
+    query_act, query_slope = swish_parts(query_pre)
+    key_act, key_slope = swish_parts(key_pre)
+    query_rot = rotate(query_act.reshape(heads_shape), cosine_table, sine_table, 1.0).astype(BF16)
+    key_rot = rotate(key_act.reshape(heads_shape), cosine_table, sine_table, 1.0).astype(BF16)
+    value_rows = value_pre.astype(BF16).reshape(heads_shape)
+    scores = jnp.einsum("ihe,jhe->hij", query_rot, key_rot, preferred_element_type=F32)
+    attn_weights = (scores * decay).astype(BF16)
+    inner_out = jnp.einsum("hij,jhe->ihe", attn_weights, value_rows, preferred_element_type=F32)
+    key_decayed = (key_rot.astype(F32) * weight_loc[:, :, None]).astype(BF16)
+    local_state = jnp.einsum("jhe,jhf->hef", key_decayed, value_rows, preferred_element_type=F32)
+    incoming = states(local_state, prefix_coef).astype(BF16)
+    outer_out = coef_in[:, :, None] * jnp.einsum("ihe,hef->ihf", query_rot, incoming, preferred_element_type=F32)
+    mixed_heads = (inner_out + outer_out).reshape(row_count, D)
+    inv_mix = lax.rsqrt(jnp.mean(mixed_heads * mixed_heads, axis=-1, keepdims=True) + EPSILON)
+    unit_mix = mixed_heads * inv_mix
+    gate_mix = (unit_mix * gate_pre).astype(BF16)
+    resid_mid = input_rows + dots(gate_mix, out_full, NN)
+    inv_second = lax.rsqrt(jnp.mean(resid_mid * resid_mid, axis=-1, keepdims=True) + EPSILON)
+    unit_second = resid_mid * inv_second
+    normed_second = unit_second.astype(BF16)
+    left_pre = dots(normed_second, left_full, NT)
+    right_pre = dots(normed_second, right_full, NT)
+    glu_product = (left_pre * right_pre).astype(BF16)
+    output = (resid_mid + dots(glu_product, down_full, NN)).astype(BF16)
+
+    product_grad = dots(glu_cot, down_full, NT)
+    left_back = (product_grad * right_pre).astype(BF16)
+    right_back = (product_grad * left_pre).astype(BF16)
+    second_back = dots(left_back, left_full, NN) + dots(right_back, right_full, NN)
+    mid_grad = glu_cot.astype(F32) + inv_second * (
+        second_back - unit_second * jnp.mean(second_back * unit_second, axis=-1, keepdims=True)
+    )
+    attn_cot = mid_grad.astype(BF16)
+    gate_mix_grad = dots(attn_cot, out_full, NT)
+    gate_back = (gate_mix_grad * unit_mix).astype(BF16)
+    unit_mix_grad = gate_mix_grad * gate_pre
+    mix_dot = jnp.mean(unit_mix_grad * unit_mix, axis=-1, keepdims=True)
+    heads_grad = (inv_mix * (unit_mix_grad - unit_mix * mix_dot)).astype(BF16).reshape(heads_shape)
+    pair_grad = jnp.einsum("ihe,jhe->hij", heads_grad, value_rows, preferred_element_type=F32).astype(BF16)
+    score_grad = (pair_grad.astype(F32) * decay).astype(BF16)
+    query_inner = jnp.einsum("hij,jhe->ihe", score_grad, key_rot, preferred_element_type=F32)
+    key_inner = jnp.einsum("hij,ihe->jhe", score_grad, query_rot, preferred_element_type=F32)
+    value_inner = jnp.einsum("hij,ihe->jhe", attn_weights, heads_grad, preferred_element_type=F32)
+    scaled_grad = (heads_grad.astype(F32) * coef_in[:, :, None]).astype(BF16)
+    query_outer = jnp.einsum("ihf,hef->ihe", scaled_grad, incoming, preferred_element_type=F32)
+    state_grad = jnp.einsum("ihe,ihf->hef", query_rot, scaled_grad, preferred_element_type=F32)
+    later_grad = states(state_grad, suffix_coef).astype(BF16)
+    key_state = weight_loc[:, :, None] * jnp.einsum("jhf,hef->jhe", value_rows, later_grad, preferred_element_type=F32)
+    value_state = weight_loc[:, :, None] * jnp.einsum("jhe,hef->jhf", key_rot, later_grad, preferred_element_type=F32)
+    query_back = (
+        rotate(query_inner + query_outer, cosine_table, sine_table, -1.0).reshape(row_count, D) * query_slope
+    ).astype(BF16)
+    key_back = (
+        rotate(key_inner + key_state, cosine_table, sine_table, -1.0).reshape(row_count, D) * key_slope
+    ).astype(BF16)
+    value_back = (value_inner + value_state).reshape(row_count, D).astype(BF16)
+    first_back = (
+        dots(query_back, query_full, NN)
+        + dots(key_back, key_full, NN)
+        + dots(value_back, value_full, NN)
+        + dots(gate_back, gate_full, NN)
+    )
+    input_back = mid_grad + inv_first * (
+        first_back - unit_first * jnp.mean(first_back * unit_first, axis=-1, keepdims=True)
+    )
+    grads = [
+        dots(glu_product, glu_cot, TN),
+        dots(left_back, normed_second, TN),
+        dots(right_back, normed_second, TN),
+        dots(gate_mix, attn_cot, TN),
+        dots(query_back, normed_first, TN),
+        dots(key_back, normed_first, TN),
+        dots(value_back, normed_first, TN),
+        dots(gate_back, normed_first, TN),
+    ]
+    sums, wholes = reduce_gradients(
+        [grad.astype(BF16).reshape(TP, -1, D) for grad in grads], [output, input_back.astype(BF16)]
+    )
+    down_grad, left_grad, right_grad, out_grad, query_grad, key_grad, value_grad, gate_grad = sums
+    return (
+        wholes[0],
+        wholes[1].astype(F32),
+        query_grad.T,
+        key_grad.T,
+        value_grad.T,
+        gate_grad.T,
+        out_grad,
+        left_grad.T,
+        right_grad.T,
+        down_grad,
+    )
+
+
 def solution(mesh):
+    fits = mesh.shape["seq"] == SEQ and mesh.shape["tp"] == TP
     return jax.shard_map(
-        body,
+        fused_body if fits else body,
         mesh=mesh,
         in_specs=(
             P(None, "seq", None),

time: 2160 us -> 668 us (0.31)
  waiting for transfers between devices: 1440 us -> 16.3 us
  Pallas kernels: 0 us -> 420 us
  other arithmetic: 181 us -> 33.6 us
  matrix products: 251 us -> 122 us
  local copies, waits for them, and re-layouts: 139 us -> 37.8 us
  blocking collectives: 107 us -> 13.4 us
    psum x4 -> x0, waiting for transfers between devices: 1090 us -> none  [the longest x2 568 us: body(): second_back = lax.psum(second_part, 'tp')]
    pallas_call x0 -> x2, Pallas kernels: none -> 420 us  [the longest x1 276 us: reduce_gradients(): pl.pallas_call(functools.partial(reduce_kernel, count, spread), out_shape...]
    reduce_scatter x8 -> x0, waiting for transfers between devices: 316 us -> none  [the longest x1 49.1 us: body(): lax.psum_scatter(accum[5], 'seq', scatter_dimension=0, tiled=True)]
    dot_general x144 -> x36, matrix products: 251 us -> 122 us  [the longest x24 93.7 us: dots(): lax.dot_general(left, right, (dims, ((), ())), preferred_element_type=F32)]
    select_n x56 -> x1, other arithmetic: 75.2 us -> 0.08 us  [fused_body(): jnp.where(((blocks > device) & (later_before == last_segment))[:, None],...]
    all_gather x5 -> x0, blocking collectives: 49.8 us -> none  [the longest x1 11.6 us: collect_weights(): lax.all_gather(query_weight, 'seq', axis=0, tiled=True)]
    mul x56 -> x0, local copies, waits for them, and re-layouts: 47.8 us -> none  [the longest x28 25 us: combine_forward(): following[0][:, None, None] * earlier[1] + following[1]]
    psum x4 -> x0, blocking collectives: 43.8 us -> none  [the longest x2 24 us: body(): total_sq = lax.psum(jnp.sum(mixed_heads * mixed_heads, axis=-1), 'tp')]
  transfers between devices with their start and end apart: 23 -> 2, of which waited for: 16 -> 1; matrix products, arithmetic and copies ran while one was open for 15% -> 6% of each run, Pallas kernels for 0% -> 0%
where the time goes in v1:
time: 668 us; the launch traced here: 659 us
  Pallas kernels  420 us (63%)
  matrix products  122 us (18%)
  local copies, waits for them, and re-layouts  37.8 us (6%)
  other arithmetic  33.6 us (5%)
  waiting for transfers between devices  16.3 us (2%)
  between operations  16.3 us (2%)
  blocking collectives  13.4 us (2%)
    pallas_call x1, Pallas kernels, reduce_gradients(): pl.pallas_call(functools.partial(reduce_kernel, count, spread), out_shape...  276 us
    pallas_call x1, Pallas kernels, gather_weights(): pl.pallas_call(functools.partial(gather_kernel, count), out_shape=[jax.Sh...  144 us
    dot_general x24, matrix products, dots(): lax.dot_general(left, right, (dims, ((), ())), preferred_element_type=F32)  93.7 us
    unnamed x132, local copies, waits for them, and re-layouts  29.2 us
    all_gather x2, waiting for transfers between devices, states(): every = lax.all_gather(local.astype(BF16), 'seq').astype(F32)  16.2 us
    unnamed x1, blocking collectives  13.4 us
  transfers between devices with their start and end apart: 2, of which 1 were waited for; matrix products, arithmetic and copies ran while one was open for 6% of the time, Pallas kernels for 0%

profile of v1, /device:TPU:0, one launch (start us, length us, event | category | flops | bytes accessed | tf_op | source)
XLA Modules:
  0.0 659.4 jit_solution(1083987682900026149)
XLA Ops:
  12.6 13.4 %all-reduce = f32[8]{0:T(128)S(1)} all-reduce(f32[8]{0:T(128)S(1)} %dynamic-update-slice), channel_id=1, replica_groups=mesh['seq'=8,'tp'=4] {'tp'}, use_global_device_ids=true, to_apply=%add | all-reduce | flops 8 | bytes 64
  34.4 144.0 %gather_weights.1 = (bf16[4,256,1024]{2,1,0:T(8,128)(2,1)}, bf16[4,256,1024]{2,1,0:T(8,128)(2,1)}, bf16[4,256,1024]{2,1,0:T(8,128)(2,1)}, bf16[4,256,1024]{2,1,0...) custom-call(bf16[256,128]{1,0:T(8,128)(2,1)} %bitcast.221, ...), custom_call_target="tpu_custom_call" | custom-call | tf_op jit(solution)/shard_map/gather_weights/pallas_call | solution.py:183
  178.4 3.4 fusion.21
  189.3 2.0 broadcast_multiply_fusion
  192.6 2.6 subtract_convert_fusion
  195.9 2.3 convolution_convert_fusion.10
  199.6 1.8 pad_maximum_fusion
  203.1 2.0 multiply_convert_fusion.1
  205.1 2.1 copy-done.2
  208.7 16.2 %all-gather.5.cloned.1.call-done = bf16[64,128,128]{2,1,0:T(8,128)(2,1)} async-done(((bf16[8,128,128]{2,1,0:T(8,128)(2,1)}), bf16[64,128,128]{2,1,0:T(8,128)(2,1)}) %all-gather.5.cloned.1.call-update) | async-done | bytes 2097168 | tf_op jit(solution)/shard_map/all_gather | solution.py:853
  224.9 2.1 fusion.1
  227.0 1.9 multiply_reduce_fusion.3
  228.9 2.3 copy.105
  231.2 3.4 multiply_convert_fusion.8
  234.7 3.0 multiply_reduce_fusion.2
  238.0 5.0 fusion.67
  243.1 5.0 fusion.66
  248.1 13.0 %multiply_convert_fusion.2 = (bf16[512,2816]{1,0:T(8,128)(2,1)}, bf16[512,2816]{1,0:T(8,128)(2,1)}, bf16[512,2816]{1,0:T(8,128)(2,1)}) fusion(f32[512,2816]{1,0:T(8,128)} %fusion.66, f32[512,2816]{1,0:T(8,128)} %fusion.67, bf16[2816,1024]{1,0:T(8,128)(2,1)} %bitcast.202, bf16[4,512,1024]{2,1,0:T(8,128)(2,1)} %param.23, s32[]{:T(128)S(6)} %select_n.26), kind=kOutput, calls=%fused_computation.3 | convolution fusion | flops 2961440768 | bytes 27000836 | tf_op jit(solution)/shard_map/dot_general | solution.py:773
  261.1 6.2 fusion.68
  267.3 5.3 multiply_reduce_fusion.1
  272.7 1.8 multiply_add_fusion.2
  274.5 2.6 convolution_convert_fusion.7
  277.1 2.6 multiply_reduce_fusion
  281.1 1.7 copy.106
  284.0 6.2 multiply_convert_fusion
  290.3 3.5 fusion.74
  295.1 4.1 convolution_convert_fusion.3
  299.1 2.8 fusion.70
  301.9 2.8 fusion.69
  304.7 6.4 convolution_convert_fusion.2
  311.1 5.0 convolution_convert_fusion
  316.1 5.4 convolution_convert_fusion.1
  321.5 4.1 add_convert_fusion.refs_8_
  325.6 2.2 fusion
  328.5 2.8 fusion.18
  332.8 2.9 fusion.73
  335.7 4.1 convolution_convert_fusion.4
  340.8 2.0 multiply_subtract_fusion
  346.5 2.7 convolution_convert_fusion.5
  352.1 2.7 convolution_convert_fusion.6
  354.9 1.7 fusion.8
  358.2 275.9 %reduce_gradients.1 = (f32[704,128]{1,0:T(8,128)}, f32[704,128]{1,0:T(8,128)}, f32[704,128]{1,0:T(8,128)}, f32[256,128]{1,0:T(8,128)}, f32[256,128]{1,0:T(8,128)...) custom-call(bf16[4,704,1024]{2,1,0:T(8,128)(2,1)} %bitcast.199, ...), custom_call_target="tpu_custom_call" | custom-call | tf_op jit(solution)/shard_map/reduce_gradients/pallas_call | solution.py:435
  634.1 1.7 copy.125
  635.7 1.7 copy.126
  637.4 1.7 copy.127
  639.0 1.7 copy.128
  640.7 6.8 %convert_element_type.291 = f32[4,512,1024]{2,1,0:T(8,128)} convert(bf16[4,512,1024]{2,1,0:T(8,128)(2,1)} %get-tuple-element.37) | non-fusion elementwise | flops 2097152 | bytes 12582912 | tf_op jit(solution)/shard_map/convert_element_type | solution.py:946
  647.5 2.0 copy.185
  (174 shorter events, 44.8 us)
Async XLA Ops:
  7.2 217.7 %all-gather.5.cloned.1.call-start = ((), (), s32[]{:S(2)}) async-start(), calls=%async_computation | async-start | bytes 2359296 | tf_op jit(solution)/shard_map/all_gather | solution.py:853
  178.4 3.4 copy-start.22
  178.4 3.8 copy-start.47
  181.8 14.1 %copy-start.19 = (bf16[64,8,8,128]{3,2,1,0:T(8,128)(2,1)}, bf16[64,8,8,128]{3,2,1,0:T(8,128)(2,1)S(1)}, u32[]{:S(2)}) copy-start(bf16[64,8,8,128]{3,2,1,0:T(8,128)(2,1)S(1)} %fusion.21) | copy-start | bytes 3145732
  183.5 3.4 copy-start.10
  195.8 6.2 copy-start.7
  198.3 127.4 %all-gather.7.cloned.1.call-start = ((), (), s32[]{:S(2)}) async-start(), calls=%async_computation.1 | async-start | bytes 2359296 | tf_op jit(solution)/shard_map/all_gather | solution.py:853
  201.8 3.2 copy-start.45
  203.1 4.1 copy-start.20
  205.1 2.1 copy-start.2
  231.2 3.4 copy-start.34
  234.6 3.0 copy-start.40
  234.6 3.3 slice-start.2
  234.6 3.3 slice-start.3
  237.7 35.0 %copy-start.14 = (f32[512,1024]{1,0:T(8,128)}, f32[512,1024]{1,0:T(8,128)S(1)}, u32[]{:S(2)}) copy-start(f32[512,1024]{1,0:T(8,128)S(1)} %get-tuple-element.112) | copy-start | bytes 6291460
  237.7 5.4 slice-start.4
  237.9 5.2 copy-start.38
  238.0 5.1 slice-start.5
  261.1 6.2 copy-start.28
  274.5 2.6 copy-start
  274.5 2.6 copy-start.35
  282.8 7.5 %copy-start.5 = (bf16[512,1024]{0,1:T(8,128)(2,1)}, bf16[512,1024]{0,1:T(8,128)(2,1)S(1)}, u32[]{:S(2)}) copy-start(bf16[512,1024]{0,1:T(8,128)(2,1)S(1)} %copy.106) | copy-start | bytes 3145732
  284.0 6.2 copy-start.8
  290.3 3.6 copy-start.6
  290.3 3.6 copy-start.31
  295.1 4.1 copy-start.3
  299.1 2.8 copy-start.4
  301.9 2.8 copy-start.26
  304.7 6.4 copy-start.29
  304.7 6.4 copy-start.39
  311.1 5.0 copy-start.27
  311.1 10.4 %slice-start = ((s8[5767168]{0:T(1024)(128)(4,1)}), s8[4194304]{0:T(1024)(128)(4,1)S(1)}, s32[]{:S(2)}) async-start(s8[5767168]{0:T(1024)(128)(4,1)} %bitcast.203), calls=%async_computation.2 | async-start | bytes 8388608
  316.1 5.4 copy-start.15
  316.1 5.4 slice-start.1
  325.6 2.9 copy-start.9
  335.6 4.1 copy-start.16
  335.7 4.1 copy-start.21
  335.7 4.1 copy-start.33
  340.8 2.0 copy-start.13
  344.3 2.2 copy-start.23
  346.5 2.7 copy-start.11
  352.1 2.7 copy-start.17
  352.1 2.7 copy-start.25
  640.7 6.8 %copy-start.18 = (bf16[4,512,1024]{2,1,0:T(8,128)(2,1)S(1)}, bf16[4,512,1024]{2,1,0:T(8,128)(2,1)}, u32[]{:S(2)}) copy-start(bf16[4,512,1024]{2,1,0:T(8,128)(2,1)} %get-tuple-element.137) | copy-start | bytes 12582916
  647.5 2.0 copy-start.46
  647.5 2.7 copy-start.44
  647.5 3.4 copy-start.43
  647.5 4.2 copy-start.42
  (11 other events, 15.5 us)
Sparse Core Ops, SparseCore 0:
  198.4 26.4 all-gather.4
  290.4 27.9 all-gather.6

commit v2 on v1

--- a/solution.py
+++ b/solution.py
@@ -21,6 +21,16 @@
 SEQ = 8
 TP = 4
 STRIPE = 128
+PAIR = 2 * HEAD
+BLOCK = 32
+
+NN = ((1,), (0,))
+NT = ((1,), (1,))
+TN = ((0,), (0,))
+
+
+def dots(left, right, dims):
+    return lax.dot_general(left, right, (dims, ((), ())), preferred_element_type=F32)
 
 
 def place():
@@ -49,159 +59,527 @@
     return pl.ds(pl.multiple_of(index * STRIPE, STRIPE), STRIPE)
 
 
-def greet(devices):
+def rows_of(index, size):
+    return pl.ds(pl.multiple_of(index * size, size), size)
+
+
+def remote(src, dst, send, receive, device):
+    return pltpu.make_async_remote_copy(
+        src_ref=src, dst_ref=dst, send_sem=send, recv_sem=receive, device_id=device, device_id_type=MESH
+    )
+
+
+def greet(s, t, around):
     barrier = pltpu.get_barrier_semaphore()
-    for device in devices:
-        pl.semaphore_signal(barrier, inc=1, device_id=device, device_id_type=MESH)
-
-
-def greet_line(t, s, here):
-    barrier = pltpu.get_barrier_semaphore()
-
-    @pl.when(t > 0)
-    def _():
-        pl.semaphore_signal(barrier, inc=1, device_id=(s, t - 1), device_id_type=MESH)
-
-    @pl.when(t < TP - 1)
-    def _():
-        pl.semaphore_signal(barrier, inc=1, device_id=(s, t + 1), device_id_type=MESH)
-
-    for device in here:
+    for step in range(1, TP):
+        pl.semaphore_signal(barrier, inc=1, device_id=(s, (t + step) % TP), device_id_type=MESH)
+    for device in around:
         pl.semaphore_signal(barrier, inc=1, device_id=(device, t), device_id_type=MESH)
-    inner = jnp.where((t > 0) & (t < TP - 1), 1, 0)
-    pl.semaphore_wait(barrier, len(here) + 1 + inner)
-
-
-SENDS = ("first", "second", "other", "relay", "relay_other", "third_other", "fourth_other")
-
-
-def gather_kernel(count, *refs):
-    ins, outs = refs[:count], refs[count : 2 * count]
-    local_sem, up_sem, down_sem, line_sem, send_sem, first_sem, second_sem, other_sem = refs[2 * count :]
+    pl.semaphore_wait(barrier, TP - 1 + len(around))
+
+
+def every_rows(count, body, size=BLOCK):
+    @pl.loop(0, count // size)
+    def _(block):
+        body(pl.ds(pl.multiple_of(block * size, size), size), block * size)
+
+
+def flag(condition):
+    return jnp.where(condition, 1.0, 0.0).astype(F32)
+
+
+def rotated(values, cosine, sine):
+    return values * cosine + pltpu.roll(values, HEAD // 2, 1) * sine
+
+
+LAG_B, LAG_C = 2, 4
+WEIGHTS = ("qkvg", "out", "left", "right", "down")
+
+
+def forward_kernel(rows, sizes, *refs):
+    (shards, refs) = refs[:5], refs[5:]
+    (hidden, cosine, sine, rate_in, bounds), refs = refs[:5], refs[5:]
+    whole_out, refs = refs[:5], refs[5:]
+    (acts_out, slope_out, normed_out, unit_out, gated_out, second_out, left_out, right_out, glu_out,
+     incoming_out, inv_mix_out, inv_second_out, rate_out, result_out), refs = refs[:14], refs[14:]
+    whole, refs = refs[:5], refs[5:]
+    (acts, slopes, normed, unit, gated, second_normed, sides, glu, wide, mixed, distance, scores, weights,
+     state, state_land, mine, partial, partial_land, incoming, inv_mix, inv_second, rates), refs = refs[:22], refs[22:]
+    (local_sem, up_sem, down_sem, line_sem, send_sem, first_sem, second_sem, other_sem, rate_send, rate_recv,
+     state_send, state_recv, partial_sem, copy_sem, side_sem) = refs
     s, t, other, first, second, diagonal = place()
-    other_first = first + (second - s) + (other - s) - (first - s)
-    other_second = second + (first - s) + (other - s) - (second - s)
-    other_diagonal = diagonal + other - s
-    greet_line(t, s, (other, first, second))
-
-    def remote(src, w, owner, column, send, receive, device):
-        return pltpu.make_async_remote_copy(
-            src_ref=src,
-            dst_ref=outs[w].at[owner, :, stripe(column)],
-            send_sem=send,
-            recv_sem=receive,
-            device_id=device,
-            device_id_type=MESH,
-        )
+    units, beside = sizes[2], wide.shape[1] // 2
+    shift = other - s
+    greet(s, t, (other, first, second, diagonal))
+
+    pairs = [(2, step) for step in range(TP)], [(3, step) for step in range(TP)]
+    items = (
+        [(0, step) for step in range(TP)]
+        + [(1, step) for step in range(TP)]
+        + [item for both in zip(*pairs) for item in both]
+        + [(4, step) for step in range(TP)]
+    )
 
     def spot(w, owner, column):
-        return outs[w].at[owner, :, stripe(column)]
-
-    waits = []
-    items = [(w, step) for w in range(count) for step in range(TP)]
-
-    def own(w):
-        return pltpu.make_async_copy(ins[w], spot(w, t, s), local_sem.at[w])
-
-    def line_copies(w, owner, src):
-        up = remote(src, w, owner, s, up_sem.at[w, owner], line_sem.at[w, owner], (s, t + 1))
-        down = remote(src, w, owner, s, down_sem.at[w, owner], line_sem.at[w, owner], (s, t - 1))
-        return up, down
-
-    def plane_copies(index, w, owner, src):
+        return whole[w].at[rows_of(owner, sizes[w]), stripe(column)]
+
+    def source(w, step, owner):
+        return shards[w] if step == 0 else spot(w, owner, s)
+
+    def up_copy(w, step, owner):
+        return remote(source(w, step, owner), spot(w, owner, s), up_sem.at[w, owner], line_sem.at[w, owner], (s, t + 1))
+
+    def down_copy(w, step, owner):
+        return remote(source(w, step, owner), spot(w, owner, s), down_sem.at[w, owner], line_sem.at[w, owner], (s, t - 1))
+
+    def own_copy(w):
+        return pltpu.make_async_copy(shards[w], spot(w, t, s), local_sem.at[w])
+
+    def plane_copies(index, w, step, owner):
+        src, dst = source(w, step, owner), spot(w, owner, s)
         return (
-            remote(src, w, owner, s, send_sem.at[index, 0], first_sem.at[index], (first, t)),
-            remote(src, w, owner, s, send_sem.at[index, 1], second_sem.at[index, 0], (second, t)),
-            remote(src, w, owner, s, send_sem.at[index, 2], other_sem.at[index, 0], (other, t)),
+            remote(src, dst, send_sem.at[index, 0], first_sem.at[index], (first, t)),
+            remote(src, dst, send_sem.at[index, 1], second_sem.at[index, 0], (second, t)),
+            remote(src, dst, send_sem.at[index, 2], other_sem.at[index, 0], (other, t)),
         )
 
     def relay_copies(index, w, owner):
         src = spot(w, owner, first)
         return (
-            remote(src, w, owner, first, send_sem.at[index, 3], second_sem.at[index, 1], (second, t)),
-            remote(src, w, owner, first, send_sem.at[index, 4], other_sem.at[index, 1], (other, t)),
+            remote(src, src, send_sem.at[index, 3], second_sem.at[index, 1], (second, t)),
+            remote(src, src, send_sem.at[index, 4], other_sem.at[index, 1], (other, t)),
         )
 
     def last_copies(index, w, owner):
+        near, far = spot(w, owner, second), spot(w, owner, diagonal)
         return (
-            remote(spot(w, owner, second), w, owner, second, send_sem.at[index, 5], other_sem.at[index, 2], (other, t)),
-            remote(spot(w, owner, diagonal), w, owner, diagonal, send_sem.at[index, 6], other_sem.at[index, 3], (other, t)),
-        )
-
-    for index in range(len(items) + 2):
+            remote(near, near, send_sem.at[index, 5], other_sem.at[index, 2], (other, t)),
+            remote(far, far, send_sem.at[index, 6], other_sem.at[index, 3], (other, t)),
+        )
+
+    def tick(now):
+        index = now
         if index < len(items):
             w, step = items[index]
             owner = nearest(t, step)
             if step == 0:
-                own(w).start()
-                src = ins[w]
-                up, down = line_copies(w, owner, src)
-                pl.when(t < TP - 1)(up.start)
-                pl.when(t > 0)(down.start)
+                own_copy(w).start()
+
+                @pl.when(t < TP - 1)
+                def _():
+                    up_copy(w, step, owner).start()
+
+                @pl.when(t > 0)
+                def _():
+                    down_copy(w, step, owner).start()
             else:
-                src = spot(w, owner, s)
-                up, down = line_copies(w, owner, src)
-                up.wait_recv()
-                pl.when((owner < t) & (t < TP - 1))(up.start)
-                pl.when((owner > t) & (t > 0))(down.start)
-            for copy in plane_copies(index, w, owner, src):
+                up_copy(w, step, owner).wait_recv()
+
+                @pl.when((owner < t) & (t < TP - 1))
+                def _():
+                    up_copy(w, step, owner).start()
+
+                @pl.when((owner > t) & (t > 0))
+                def _():
+                    down_copy(w, step, owner).start()
+            for copy in plane_copies(index, w, step, owner):
                 copy.start()
-        if 1 <= index <= len(items):
-            w, step = items[index - 1]
+        index = now - LAG_B
+        if 0 <= index < len(items):
+            w, step = items[index]
             owner = nearest(t, step)
-            remote(spot(w, owner, first), w, owner, first, send_sem.at[index - 1, 0], first_sem.at[index - 1], (first, t)).wait_recv()
-            for copy in relay_copies(index - 1, w, owner):
+            here = spot(w, owner, first)
+            remote(here, here, send_sem.at[index, 0], first_sem.at[index], (first, t)).wait_recv()
+            for copy in relay_copies(index, w, owner):
                 copy.start()
-        if index >= 2:
-            w, step = items[index - 2]
+        index = now - LAG_C
+        if 0 <= index < len(items):
+            w, step = items[index]
             owner = nearest(t, step)
             for part, column in enumerate((second, diagonal)):
-                remote(spot(w, owner, column), w, owner, column, send_sem.at[index - 2, 1], second_sem.at[index - 2, part], (second, t)).wait_recv()
-            for copy in last_copies(index - 2, w, owner):
+                here = spot(w, owner, column)
+                remote(here, here, send_sem.at[index, 1], second_sem.at[index, part], (second, t)).wait_recv()
+            for copy in last_copies(index, w, owner):
                 copy.start()
+
+    keeps = []
+
+    def keep(src, dst):
+        copy = functools.partial(pltpu.make_async_copy, src, dst, copy_sem.at[len(keeps)])
+        copy().start()
+        keeps.append(copy)
+
+    def ready(index):
+        w, step = items[index]
+        owner = nearest(t, step)
+        if step == 0:
+            own_copy(w).wait()
+        for part, column in enumerate((other, second + shift, first + shift, diagonal + shift)):
+            here = spot(w, owner, column)
+            remote(here, here, send_sem.at[index, 2], other_sem.at[index, part], (other, t)).wait_recv()
+        block = rows_of(owner, sizes[w])
+        keep(whole[w].at[block, :], whole_out[w].at[block, :])
+        return owner, block
+
+    def rate_copy(step):
+        return remote(rate_in, rates.at[t], rate_send.at[step - 1], rate_recv.at[step - 1], (s, (t + step) % TP))
+
+    for step in range(1, TP):
+        rate_copy(step).start()
+    rates[t] = rate_in[...]
+
+    tick(0)
+    tick(1)
+    boundary = bounds[t]
+    edge = boundary - s * rows
+
+    def prepare(part, start):
+        values = hidden[part, :].astype(F32)
+        scale = lax.rsqrt(jnp.mean(values * values, axis=-1, keepdims=True) + EPSILON)
+        normed[part, :] = (values * scale).astype(BF16)
+        row = lax.broadcasted_iota(jnp.int32, (BLOCK, rows), 0) + start
+        column = lax.broadcasted_iota(jnp.int32, (BLOCK, rows), 1)
+        apart = (column > row) | ((row >= edge) & (column < edge))
+        distance[part, :] = jnp.where(apart, -1, row - column).astype(F32)
+
+    every_rows(rows, prepare)
+    keep(normed, normed_out)
+    for step in range(1, TP):
+        here = rates.at[t]
+        remote(here, here, rate_send.at[step - 1], rate_recv.at[step - 1], (s, t)).wait_recv()
+    keep(rates, rate_out)
+
+    before = jnp.where(s * rows - 1 >= boundary, 1, 0)
+    last = jnp.where(s * rows + rows - 1 >= boundary, 1, 0)
+
+    def rate_of(block, half):
+        return rates[block, half : half + 1, :]
+
+    def row_numbers(start, count=BLOCK):
+        return lax.broadcasted_iota(jnp.int32, (count, HEAD), 0) + start
+
+    def project(index):
+        owner, block = ready(index)
+        wide[:, 0:D] = dots(normed[...], whole[0][block, :], NT)
+
+        def shape_rows(part, start):
+            turn, lean = cosine[part, :], sine[part, :]
+            for kind in range(2):
+                for half in range(2):
+                    at = kind * PAIR + half * HEAD
+                    values = wide[part, at : at + HEAD]
+                    logistic = 1.0 / (1.0 + jnp.exp(-values))
+                    acts[owner, part, at : at + HEAD] = rotated(values * logistic, turn, lean).astype(BF16)
+                    slopes[owner, part, at : at + HEAD] = (
+                        logistic * (1.0 + values * (1.0 - logistic))
+                    ).astype(BF16)
+            acts[owner, part, 2 * PAIR : 4 * PAIR] = wide[part, 2 * PAIR : 4 * PAIR].astype(BF16)
+            number = row_numbers(start)
+            valid = jnp.where(jnp.where(number >= edge, 1, 0) == last, 1.0, 0.0)
+            for half in range(2):
+                fade = jnp.exp(-rate_of(owner, half) * (rows - 1 - number).astype(F32)) * valid
+                keys = acts[owner, part, PAIR + half * HEAD : PAIR + half * HEAD + HEAD].astype(F32)
+                weights[part, half * HEAD : half * HEAD + HEAD] = (keys * fade).astype(BF16)
+
+        every_rows(rows, shape_rows)
+        for half in range(2):
+            at = half * HEAD
+            state[owner * 2 + half] = dots(
+                weights[:, at : at + HEAD], acts[owner, :, 2 * PAIR + at : 2 * PAIR + at + HEAD], TN
+            ).astype(BF16)
+
+    def attend(step):
+        owner = nearest(t, step)
+        for half in range(2):
+            at = half * HEAD
+            rate = rates[owner, half : half + 1, :]
+            for top in range(0, rows, PAIR):
+                width = top + PAIR
+                scores[0:PAIR, 0:width] = dots(
+                    acts[owner, top : top + PAIR, at : at + HEAD], acts[owner, 0:width, PAIR + at : PAIR + at + HEAD], NT
+                )
+
+                def weigh(part, start, width=width, top=top, rate=rate):
+                    for left in range(0, width, HEAD):
+                        apart = distance[pl.ds(pl.multiple_of(start + top, BLOCK), BLOCK), left : left + HEAD]
+                        fade = jnp.where(apart >= 0.0, jnp.exp(-rate * apart), 0.0)
+                        weights[part, left : left + HEAD] = (scores[part, left : left + HEAD] * fade).astype(BF16)
+
+                every_rows(PAIR, weigh)
+                column = pl.ds(pl.multiple_of(owner * PAIR + at, HEAD), HEAD)
+                mixed[top : top + PAIR, column] = dots(
+                    weights[0:PAIR, 0:width], acts[owner, 0:width, 2 * PAIR + at : 2 * PAIR + at + HEAD], NN
+                )
+
+    around = (first, second, diagonal)
+
+    def state_copy(part):
+        return remote(state, state_land.at[part], state_send.at[part], state_recv.at[part], (around[part], t))
+
+    def prefix_scale(block, source_block, rate):
+        same = jnp.where((source_block + 1) * rows - 1 >= boundary, 1, 0) == jnp.where(block * rows - 1 >= boundary, 1, 0)
+        usable = flag(source_block < block) * flag(same)
+        gap = jnp.maximum(block - 1 - source_block, 0).astype(F32)
+        return jnp.exp(-rate * (rows * gap)) * usable
+
+    def partial_copy():
+        return remote(partial, partial_land, partial_sem.at[0], partial_sem.at[1], (other, t))
+
+    def collect():
+        for part in range(3):
+            state_copy(part).wait_recv()
+
+        @pl.loop(0, 2 * TP)
+        def _(head):
+            rate = rates[head // 2, pl.ds(head % 2, 1), :]
+            here = jnp.zeros((HEAD, HEAD), F32)
+            there = prefix_scale(other, s, rate) * state[head].astype(F32)
+            for part in range(3):
+                values = state_land[part, head].astype(F32)
+                here += prefix_scale(s, around[part], rate) * values
+                there += prefix_scale(other, around[part], rate) * values
+            mine[head] = here
+            partial[head] = there
+
+        partial_copy().start()
+
+    def mix():
+        partial_copy().wait_recv()
+
+        @pl.loop(0, 2 * TP)
+        def _(head):
+            incoming[head] = (mine[head] + partial_land[head]).astype(BF16)
+
+        keep(incoming, incoming_out)
+        for block in range(TP):
+            for half in range(2):
+                at = half * HEAD
+                scores[:, at : at + HEAD] = dots(acts[block, :, at : at + HEAD], incoming[2 * block + half], NN)
+
+            def add_outer(part, start, block=block):
+                number = row_numbers(start)
+                valid = jnp.where(jnp.where(number >= edge, 1, 0) == before, 1.0, 0.0)
+                for half in range(2):
+                    fade = jnp.exp(-rate_of(block, half) * (number + 1).astype(F32)) * valid
+                    column = slice(block * PAIR + half * HEAD, block * PAIR + half * HEAD + HEAD)
+                    mixed[part, column] += fade * scores[part, half * HEAD : half * HEAD + HEAD]
+
+            every_rows(rows, add_outer)
+
+        def gate_rows(part, start):
+            values = mixed[part, :]
+            scale = lax.rsqrt(jnp.mean(values * values, axis=-1, keepdims=True) + EPSILON)
+            inv_mix[part, :] = jnp.broadcast_to(scale, (BLOCK, HEAD))
+            values = values * scale
+            unit[part, :] = values.astype(BF16)
+            for block in range(TP):
+                column = slice(block * PAIR, block * PAIR + PAIR)
+                gate = acts[block, part, 3 * PAIR : 4 * PAIR].astype(F32)
+                gated[part, column] = (values[:, column] * gate).astype(BF16)
+
+        every_rows(rows, gate_rows, BLOCK)
+        keep(acts, acts_out)
+        keep(slopes, slope_out)
+        keep(unit, unit_out)
+        keep(gated, gated_out)
+        keep(inv_mix, inv_mix_out)
+
+    def project_out():
+        wide[:, 0:D] = dots(gated[...], whole[1][...], NN)
+
+        def norm_rows(part, start):
+            values = hidden[part, :].astype(F32) + wide[part, 0:D]
+            mixed[part, :] = values
+            scale = lax.rsqrt(jnp.mean(values * values, axis=-1, keepdims=True) + EPSILON)
+            inv_second[part, :] = jnp.broadcast_to(scale, (BLOCK, HEAD))
+            second_normed[part, :] = (values * scale).astype(BF16)
+
+        every_rows(rows, norm_rows)
+        keep(second_normed, second_out)
+        keep(inv_second, inv_second_out)
+
+    def left_side(index):
+        owner, block = ready(index)
+        wide[:, 0:units] = dots(second_normed[...], whole[2][block, :], NT)
+
+    def side_copies(slot, owner):
+        return (
+            pltpu.make_async_copy(sides.at[slot, 0], left_out.at[owner], side_sem.at[slot, 0]),
+            pltpu.make_async_copy(sides.at[slot, 1], right_out.at[owner], side_sem.at[slot, 1]),
+        )
+
+    def right_side(index):
+        owner, block = ready(index)
+        wide[:, beside : beside + units] = dots(second_normed[...], whole[3][block, :], NT)
+        step = items[index][1]
+        slot = step % 2
+        if step >= 2:
+            for copy in side_copies(slot, nearest(t, step - 2)):
+                copy.wait()
+
+        def multiply(part, start):
+            left, right = wide[part, 0:units], wide[part, beside : beside + units]
+            glu[owner, part, :] = (left * right).astype(BF16)
+            sides[slot, 0, part, :] = left.astype(BF16)
+            sides[slot, 1, part, :] = right.astype(BF16)
+
+        every_rows(rows, multiply)
+        for copy in side_copies(slot, owner):
+            copy.start()
+        keep(glu.at[owner], glu_out.at[owner])
+
+    def down(index):
+        owner, block = ready(index)
+        mixed[...] += dots(glu[owner], whole[4][block, :], NN)
+
+    for now in range(2, 6):
+        tick(now)
+    for step in range(TP):
+        project(step)
+        tick(6 + step)
+    for part in range(3):
+        state_copy(part).start()
+    for step in range(TP):
+        attend(step)
+        if step < 2:
+            tick(10 + step)
+    collect()
+    for index in range(TP, 2 * TP):
+        ready(index)
+    tick(12)
+    mix()
+    tick(13)
+    project_out()
+    for index in range(2 * TP, len(items)):
+        if index + 6 < len(items) + LAG_C:
+            tick(index + 6)
+        w = items[index][0]
+        (left_side, right_side, down)[w - 2](index)
+
+    def finish(part, start):
+        result_out[part, :] = mixed[part, :].astype(BF16)
+
+    every_rows(rows, finish)
+
+    for step in range(1, TP):
+        rate_copy(step).wait_send()
+    for part in range(3):
+        state_copy(part).wait_send()
+    partial_copy().wait_send()
+    for copy in keeps:
+        copy().wait()
+    for step in (2, 3):
+        for copy in side_copies(step % 2, nearest(t, step)):
+            copy.wait()
     for index, (w, step) in enumerate(items):
         owner = nearest(t, step)
-        for part, column in enumerate((other, other_first, other_second, other_diagonal)):
-            remote(spot(w, owner, column), w, owner, column, send_sem.at[index, 2], other_sem.at[index, part], (other, t)).wait_recv()
-        src = ins[w] if step == 0 else spot(w, owner, s)
-        up, down = line_copies(w, owner, src)
         if step == 0:
-            own(w).wait()
-            pl.when(t < TP - 1)(up.wait_send)
-            pl.when(t > 0)(down.wait_send)
+
+            @pl.when(t < TP - 1)
+            def _():
+                up_copy(w, step, owner).wait_send()
+
+            @pl.when(t > 0)
+            def _():
+                down_copy(w, step, owner).wait_send()
         else:
-            pl.when((owner < t) & (t < TP - 1))(up.wait_send)
-            pl.when((owner > t) & (t > 0))(down.wait_send)
-        for copy in plane_copies(index, w, owner, src) + relay_copies(index, w, owner) + last_copies(index, w, owner):
+
+            @pl.when((owner < t) & (t < TP - 1))
+            def _():
+                up_copy(w, step, owner).wait_send()
+
+            @pl.when((owner > t) & (t > 0))
+            def _():
+                down_copy(w, step, owner).wait_send()
+        for copy in plane_copies(index, w, step, owner) + relay_copies(index, w, owner) + last_copies(index, w, owner):
             copy.wait_send()
 
 
-def gather_weights(shards):
-    count = len(shards)
-    items = count * TP
+KEPT = 34
+
+
+def forward(shards, hidden, cosine, sine, rate, bounds):
+    rows = hidden.shape[0]
+    sizes = tuple(shard.shape[0] for shard in shards)
+    units = sizes[2]
+    beside = -(-units // HEAD) * HEAD
+    items = 5 * TP
     dma = pltpu.SemaphoreType.DMA
+    vmem = pl.BlockSpec(memory_space=pltpu.VMEM)
+    anywhere = pl.BlockSpec(memory_space=pl.ANY)
+    heads = 2 * TP
+    outs = [jax.ShapeDtypeStruct((TP * size, D), BF16) for size in sizes] + [
+        jax.ShapeDtypeStruct((TP, rows, 4 * PAIR), BF16),
+        jax.ShapeDtypeStruct((TP, rows, 2 * PAIR), BF16),
+        jax.ShapeDtypeStruct((rows, D), BF16),
+        jax.ShapeDtypeStruct((rows, D), BF16),
+        jax.ShapeDtypeStruct((rows, D), BF16),
+        jax.ShapeDtypeStruct((rows, D), BF16),
+        jax.ShapeDtypeStruct((TP, rows, units), BF16),
+        jax.ShapeDtypeStruct((TP, rows, units), BF16),
+        jax.ShapeDtypeStruct((TP, rows, units), BF16),
+        jax.ShapeDtypeStruct((heads, HEAD, HEAD), BF16),
+        jax.ShapeDtypeStruct((rows, HEAD), F32),
+        jax.ShapeDtypeStruct((rows, HEAD), F32),
+        jax.ShapeDtypeStruct((TP, 8, HEAD), F32),
+        jax.ShapeDtypeStruct((rows, D), BF16),
+    ]
     return pl.pallas_call(
-        functools.partial(gather_kernel, count),
-        out_shape=[jax.ShapeDtypeStruct((TP, shard.shape[0], D), BF16) for shard in shards],
-        in_specs=[pl.BlockSpec(memory_space=pl.ANY)] * count,
-        out_specs=[pl.BlockSpec(memory_space=pl.ANY)] * count,
-        scratch_shapes=[
-            dma((count,)),
-            dma((count, TP)),
-            dma((count, TP)),
-            dma((count, TP)),
+        functools.partial(forward_kernel, rows, sizes),
+        out_shape=outs,
+        in_specs=[anywhere] * 5 + [vmem] * 4 + [pl.BlockSpec(memory_space=pltpu.SMEM)],
+        out_specs=[anywhere] * (len(outs) - 1) + [vmem],
+        scratch_shapes=[pltpu.VMEM((TP * size, D), BF16) for size in sizes]
+        + [
+            pltpu.VMEM((TP, rows, 4 * PAIR), BF16),
+            pltpu.VMEM((TP, rows, 2 * PAIR), BF16),
+            pltpu.VMEM((rows, D), BF16),
+            pltpu.VMEM((rows, D), BF16),
+            pltpu.VMEM((rows, D), BF16),
+            pltpu.VMEM((rows, D), BF16),
+            pltpu.VMEM((2, 2, rows, units), BF16),
+            pltpu.VMEM((TP, rows, units), BF16),
+            pltpu.VMEM((rows, max(2 * beside, D)), F32),
+            pltpu.VMEM((rows, D), F32),
+            pltpu.VMEM((rows, rows), F32),
+            pltpu.VMEM((rows, rows), F32),
+            pltpu.VMEM((rows, rows), BF16),
+            pltpu.VMEM((heads, HEAD, HEAD), BF16),
+            pltpu.VMEM((3, heads, HEAD, HEAD), BF16),
+            pltpu.VMEM((heads, HEAD, HEAD), F32),
+            pltpu.VMEM((heads, HEAD, HEAD), F32),
+            pltpu.VMEM((heads, HEAD, HEAD), F32),
+            pltpu.VMEM((heads, HEAD, HEAD), BF16),
+            pltpu.VMEM((rows, HEAD), F32),
+            pltpu.VMEM((rows, HEAD), F32),
+            pltpu.VMEM((TP, 8, HEAD), F32),
+            dma((5,)),
+            dma((5, TP)),
+            dma((5, TP)),
+            dma((5, TP)),
             dma((items, 7)),
             dma((items,)),
             dma((items, 2)),
             dma((items, 4)),
+            dma((TP - 1,)),
+            dma((TP - 1,)),
+            dma((3,)),
+            dma((3,)),
+            dma((2,)),
+            dma((KEPT,)),
+            dma((2, 2)),
         ],
-        compiler_params=pltpu.CompilerParams(collective_id=0, has_side_effects=True),
-        name="gather_weights",
-    )(*shards)
+        compiler_params=pltpu.CompilerParams(
+            collective_id=0, has_side_effects=True, vmem_limit_bytes=60 * 2**20
+        ),
+        name="forward",
+    )(*shards, hidden, cosine, sine, rate, bounds)
 
 
 ROWS_STEP = 64
 PIECES = 4
+LAG_1, LAG_2, LAG_3, LAG_4 = 2, 4, 6, 8
+SLOTS = 4
 
 
 def add_rows(target, *terms):
@@ -231,12 +609,7 @@
      line_send, below_recv, above_recv, share_local, share_up, share_down, share_recv) = refs
     s, t, other, first, second, diagonal = place()
     core = s % 2
-    greet_line(t, s, (other, first, second))
-
-    def remote(src, dst, send, receive, device):
-        return pltpu.make_async_remote_copy(
-            src_ref=src, dst_ref=dst, send_sem=send, recv_sem=receive, device_id=device, device_id_type=MESH
-        )
+    greet(s, t, (other, first, second))
 
     piece_rows = shares[0].shape[0] // PIECES
     pieces = [(a, p) for p in range(PIECES) for a in range(spread)]
@@ -323,14 +696,14 @@
         return up, down
 
     total = len(items)
-    for tick in range(total + 4):
+    for tick in range(total + LAG_4):
         index = tick
         if index < total:
             w, step = items[index]
             owner = nearest(t, step)
             for copy in sends(index, w, owner) + loads(index, w, owner):
                 copy.start()
-        index = tick - 1
+        index = tick - LAG_1
         if 0 <= index < total:
             w, step = items[index]
             owner = nearest(t, step)
@@ -347,7 +720,7 @@
                 )
             for copy in to_second(index, w, owner):
                 copy.start()
-        index = tick - 2
+        index = tick - LAG_2
         if 0 <= index < total:
             w, step = items[index]
             owner = nearest(t, step)
@@ -355,7 +728,7 @@
                 copy.wait_recv()
             add_rows(second_land[w].at[owner, 0], second_land[w].at[owner, 0], other_land[w].at[owner, first // 2])
             to_first(index, w, owner).start()
-        index = tick - 3
+        index = tick - LAG_3
         if 0 <= index < total:
             w, step = items[index]
             owner = nearest(t, step)
@@ -366,7 +739,7 @@
                 other_land[w].at[owner, s // 2],
                 second_land[w].at[owner, 1],
             )
-        index = tick - 4
+        index = tick - LAG_4
         if 0 <= index < total:
             w, step = items[index]
             owner = nearest(t, step)
@@ -438,14 +811,14 @@
         + [jax.ShapeDtypeStruct((TP, *share.shape), share.dtype) for share in shares],
         in_specs=[anywhere] * (count + spread),
         out_specs=[vmem] * count + [anywhere] * spread,
-        scratch_shapes=[pltpu.VMEM((3, 4, max(rows), STRIPE), BF16)]
+        scratch_shapes=[pltpu.VMEM((SLOTS, 4, max(rows), STRIPE), BF16)]
         + [pltpu.VMEM((TP, 4, r, STRIPE), BF16) for r in rows]
         + [pltpu.VMEM((TP, 2, r, STRIPE), BF16) for r in rows]
         + [pltpu.VMEM((TP, r, STRIPE), BF16) for r in rows]
         + [pltpu.VMEM((TP, r, STRIPE), BF16) for r in rows]
         + [pltpu.VMEM((TP, r, STRIPE), BF16) for r in rows]
         + [
-            dma((3, 4)),
+            dma((SLOTS, 4)),
             dma((items, 4)),
             dma((items, 4)),
             dma((items, 2)),
@@ -769,15 +1142,6 @@
     )
 
 
-def dots(left, right, dims):
-    return lax.dot_general(left, right, (dims, ((), ())), preferred_element_type=F32)
-
-
-NN = ((1,), (0,))
-NT = ((1,), (1,))
-TN = ((0,), (0,))
-
-
 def fused_body(
     hidden_in,
     query_weight,
@@ -794,21 +1158,16 @@
 ):
     row_count = hidden_in.shape[1]
     device, batch = lax.axis_index("seq"), lax.axis_index("tp")
-    rates = lax.all_gather(decay_rate, "tp", axis=0, tiled=True)
-    heads = rates.shape[0]
+    rates = None
+    units = left_weight.shape[1]
     shards = [
-        query_weight.T,
-        key_weight.T,
-        value_weight.T,
-        gate_weight.T,
+        jnp.concatenate([query_weight.T, key_weight.T, value_weight.T, gate_weight.T], axis=0),
         out_weight,
         left_weight.T,
         right_weight.T,
         down_weight,
     ]
-    query_full, key_full, value_full, gate_full, out_full, left_full, right_full, down_full = [
-        whole.reshape(-1, D) for whole in gather_weights(shards)
-    ]
+    heads = 2 * TP
     heads_shape = (row_count, heads, HEAD)
     offsets = jnp.arange(row_count, dtype=jnp.int32)
     positions = device * row_count + offsets
@@ -816,8 +1175,22 @@
         jnp.arange(HEAD // 2, dtype=F32) * (-2.0 * math.log(10000.0) / HEAD)
     )
     angles = positions.astype(F32)[:, None] * frequency[None, :]
-    cosine_table = jnp.cos(angles)[:, None, :]
-    sine_table = jnp.sin(angles)[:, None, :]
+    cosine, sine = jnp.cos(angles), jnp.sin(angles)
+    cosine_table, sine_table = cosine[:, None, :], sine[:, None, :]
+    input_bf = lax.dynamic_index_in_dim(hidden_in, batch, 0, keepdims=False)
+    glu_cot = lax.dynamic_index_in_dim(out_cotangent, batch, 0, keepdims=False)
+    results = forward(
+        shards,
+        input_bf,
+        jnp.concatenate([cosine, cosine], axis=1),
+        jnp.concatenate([-sine, sine], axis=1),
+        jnp.broadcast_to(jnp.pad(decay_rate, (0, 6))[:, None], (8, HEAD)),
+        seq_bounds,
+    )
+    qkvg_full, out_full, left_full, right_full, down_full = results[:5]
+    (acts, slopes, normed_first, unit_mix, gate_mix, normed_second, left_pre, right_pre, glu_parts, incoming,
+     inv_mix, inv_second, rates, output) = results[5:]
+    rates = rates[:, :2, 0].reshape(heads)
     local_f = offsets.astype(F32)
     distance = local_f[:, None] - local_f[None, :]
     boundary = lax.dynamic_index_in_dim(seq_bounds, batch, 0, keepdims=False)
@@ -853,39 +1226,26 @@
         every = lax.all_gather(local.astype(BF16), "seq").astype(F32)
         return jnp.sum(coef[:, :, None, None] * every, axis=0)
 
-    input_rows = lax.dynamic_index_in_dim(hidden_in, batch, 0, keepdims=False).astype(F32)
-    glu_cot = lax.dynamic_index_in_dim(out_cotangent, batch, 0, keepdims=False)
+    def side(parts):
+        return parts.transpose(1, 0, 2).reshape(row_count, -1)
+
+    def kind(parts, index, size):
+        return side(parts[:, :, index * size : index * size + size])
+
+    query_rot, key_rot, value_rows = [kind(acts, index, PAIR).reshape(heads_shape) for index in range(3)]
+    gate_pre = kind(acts, 3, PAIR).astype(F32)
+    query_slope, key_slope = [kind(slopes, index, PAIR).astype(F32) for index in range(2)]
+    query_full, key_full, value_full, gate_full = [
+        qkvg_full.reshape(TP, 4, PAIR, D)[:, index].reshape(D, D) for index in range(4)
+    ]
+    left_pre, right_pre, glu_product = side(left_pre).astype(F32), side(right_pre).astype(F32), side(glu_parts)
+    inv_mix, inv_second = inv_mix[:, :1], inv_second[:, :1]
+    unit_mix, unit_second = unit_mix.astype(F32), normed_second.astype(F32)
+    input_rows = input_bf.astype(F32)
     inv_first = lax.rsqrt(jnp.mean(input_rows * input_rows, axis=-1, keepdims=True) + EPSILON)
     unit_first = input_rows * inv_first
-    normed_first = unit_first.astype(BF16)
-    query_pre = dots(normed_first, query_full, NT)
-    key_pre = dots(normed_first, key_full, NT)
-    value_pre = dots(normed_first, value_full, NT)
-    gate_pre = dots(normed_first, gate_full, NT)
-    query_act, query_slope = swish_parts(query_pre)
-    key_act, key_slope = swish_parts(key_pre)
-    query_rot = rotate(query_act.reshape(heads_shape), cosine_table, sine_table, 1.0).astype(BF16)
-    key_rot = rotate(key_act.reshape(heads_shape), cosine_table, sine_table, 1.0).astype(BF16)
-    value_rows = value_pre.astype(BF16).reshape(heads_shape)
     scores = jnp.einsum("ihe,jhe->hij", query_rot, key_rot, preferred_element_type=F32)
     attn_weights = (scores * decay).astype(BF16)
-    inner_out = jnp.einsum("hij,jhe->ihe", attn_weights, value_rows, preferred_element_type=F32)
-    key_decayed = (key_rot.astype(F32) * weight_loc[:, :, None]).astype(BF16)
-    local_state = jnp.einsum("jhe,jhf->hef", key_decayed, value_rows, preferred_element_type=F32)
-    incoming = states(local_state, prefix_coef).astype(BF16)
-    outer_out = coef_in[:, :, None] * jnp.einsum("ihe,hef->ihf", query_rot, incoming, preferred_element_type=F32)
-    mixed_heads = (inner_out + outer_out).reshape(row_count, D)
-    inv_mix = lax.rsqrt(jnp.mean(mixed_heads * mixed_heads, axis=-1, keepdims=True) + EPSILON)
-    unit_mix = mixed_heads * inv_mix
-    gate_mix = (unit_mix * gate_pre).astype(BF16)
-    resid_mid = input_rows + dots(gate_mix, out_full, NN)
-    inv_second = lax.rsqrt(jnp.mean(resid_mid * resid_mid, axis=-1, keepdims=True) + EPSILON)
-    unit_second = resid_mid * inv_second
-    normed_second = unit_second.astype(BF16)
-    left_pre = dots(normed_second, left_full, NT)
-    right_pre = dots(normed_second, right_full, NT)
-    glu_product = (left_pre * right_pre).astype(BF16)
-    output = (resid_mid + dots(glu_product, down_full, NN)).astype(BF16)
 
     product_grad = dots(glu_cot, down_full, NT)
     left_back = (product_grad * right_pre).astype(BF16)

time: 668 us -> 618 us (0.925)
  matrix products: 122 us -> 77.5 us
  local copies, waits for them, and re-layouts: 37.8 us -> 67 us
  Pallas kernels: 420 us -> 401 us
  waiting for transfers between devices: 16.3 us -> 0.04 us
  blocking collectives: 13.4 us -> 0 us
  other arithmetic: 33.6 us -> 44.6 us
    dot_general x24 -> x16, matrix products: 93.7 us -> 57.6 us  [dots(): lax.dot_general(left, right, (dims, ((), ())), preferred_element_type=F32)]
    convert_element_type x2 -> x7, local copies, waits for them, and re-layouts: 3.15 us -> 29.7 us  [the longest x2 12.9 us: fused_body(): side(left_pre).astype(F32)]
    pallas_call x1, Pallas kernels: 276 us -> 256 us  [reduce_gradients(): pl.pallas_call(functools.partial(reduce_kernel, count, spread), out_shape...]
    all_gather x2 -> x1, waiting for transfers between devices: 16.2 us -> 0.02 us  [states(): every = lax.all_gather(local.astype(BF16), 'seq').astype(F32)]
    unnamed x1 -> x0, blocking collectives: 13.4 us -> none
    convert_element_type x2 -> x3, other arithmetic: 1.52 us -> 11.6 us  [the longest x1 5.13 us: fused_body(): side(right_pre).astype(F32)]
    transpose x0 -> x4, local copies, waits for them, and re-layouts: none -> 8.95 us  [side(): return parts.transpose(1, 0, 2).reshape(row_count, -1)]
    dot_general x4 -> x0, matrix products: 7.71 us -> none  [the longest x1 2.32 us: fused_body(): jnp.einsum('jhe,jhf->hef', key_decayed, value_rows, preferred_element_typ...]
  transfers between devices with their start and end apart: 2 -> 1, of which waited for: 1 -> 0; matrix products, arithmetic and copies ran while one was open for 6% -> 11% of each run, Pallas kernels for 0% -> 0%
where the time goes in v2:
time: 618 us; the launch traced here: 606 us
  Pallas kernels  401 us (65%)
  matrix products  77.5 us (13%)
  local copies, waits for them, and re-layouts  67 us (11%)
  other arithmetic  44.6 us (7%)
  between operations  15.7 us (3%)
    pallas_call x1, Pallas kernels, reduce_gradients(): pl.pallas_call(functools.partial(reduce_kernel, count, spread), out_shape...  256 us
    pallas_call x1, Pallas kernels, forward(): pl.pallas_call(functools.partial(forward_kernel, rows, sizes), out_shape=...  145 us
    dot_general x16, matrix products, dots(): lax.dot_general(left, right, (dims, ((), ())), preferred_element_type=F32)  57.6 us
    unnamed x141, local copies, waits for them, and re-layouts  21.5 us
    convert_element_type x2, local copies, waits for them, and re-layouts, fused_body(): side(left_pre).astype(F32)  12.9 us
    convert_element_type x2, local copies, waits for them, and re-layouts, fused_body(): side(right_pre).astype(F32)  12.8 us
  transfers between devices with their start and end apart: 1, of which 0 were waited for; matrix products, arithmetic and copies ran while one was open for 11% of the time, Pallas kernels for 0%

profile of v2, /device:TPU:0, one launch (start us, length us, event | category | flops | bytes accessed | tf_op | source)
XLA Modules:
  0.0 606.0 jit_solution(9683977878841561140)
XLA Ops:
  11.1 3.0 fusion.19
  14.7 1.8 fusion.46
  18.8 145.2 %forward.1 = (bf16[4096,1024]{1,0:T(8,128)(2,1)}, bf16[1024,1024]{1,0:T(8,128)(2,1)}, bf16[2816,1024]{1,0:T(8,128)(2,1)}, bf16[2816,1024]{1,0:T(8,128)(2,1)}, bf...) custom-call(bf16[1024,128]{1,0:T(8,128)(2,1)} %pad_maximum_fusion.2., ...), custom_call_target="tpu_custom_call" | custom-call | tf_op jit(solution)/shard_map/forward/pallas_call | solution.py:527
  164.0 5.1 convert_bitcast_fusion.1
  169.1 6.4 %copy.106 = f32[512,4,704]{0,2,1:T(8,128)} copy(f32[512,4,704]{2,0,1:T(8,128)} %convert_bitcast_fusion.1) | data formatting | bytes 11534336 | tf_op jit(solution)/shard_map/convert_element_type | solution.py:1241
  175.6 6.4 %copy.107 = f32[512,2816]{1,0:T(8,128)} copy(f32[512,2816]{0,1:T(8,128)} %bitcast.147) | data formatting | bytes 11534336 | tf_op jit(solution)/shard_map/convert_element_type | solution.py:1241
  181.9 3.2 convert_bitcast_fusion
  185.2 6.4 %copy.108 = f32[512,4,704]{0,2,1:T(8,128)} copy(f32[512,4,704]{2,0,1:T(8,128)} %convert_bitcast_fusion) | data formatting | bytes 11534336 | tf_op jit(solution)/shard_map/convert_element_type | solution.py:1241
  191.6 6.5 %copy.109 = f32[512,2816]{1,0:T(8,128)} copy(f32[512,2816]{0,1:T(8,128)} %bitcast.148) | data formatting | bytes 11534336 | tf_op jit(solution)/shard_map/convert_element_type | solution.py:1241
  198.1 9.6 %multiply_convert_fusion.2 = (bf16[512,2816]{1,0:T(8,128)(2,1)S(1)}, bf16[512,2816]{1,0:T(8,128)(2,1)S(1)}) fusion(f32[512,2816]{1,0:T(8,128)} %copy.109, f32[512,2816]{1,0:T(8,128)} %copy.107, bf16[2816,1024]{1,0:T(8,128)(2,1)} %get-tuple-element.40, bf16[4,512,1024]{2,1,0:T(8,128)(2,1)} %param.23, s32[]{:T(128)S(6)} %select_n.19), kind=kOutput, calls=%fused_computation.5 | convolution fusion | flops 2958557184 | bytes 24117252 | tf_op jit(solution)/shard_map/dot_general | solution.py:33
  207.7 3.1 fusion.61
  210.9 5.5 fusion.15
  216.6 1.8 slice_bitcast_fusion
  218.7 1.9 fusion.18
  221.0 2.7 fusion.20
  226.6 1.3 compare_convert_fusion.1
  227.9 2.3 copy.119
  231.6 1.8 convolution_convert_fusion.8
  236.1 1.9 compare_and_fusion
  238.6 1.3 copy.112
  241.3 3.2 convert_bitcast_fusion.2
  244.5 1.9 copy.121
  246.4 1.9 copy.118
  248.9 4.8 copy.105
  253.7 4.0 multiply_convert_fusion.1
  257.7 1.5 fusion.62
  259.3 2.2 add_bitcast_fusion
  262.2 2.7 convolution_convert_fusion.3
  265.6 2.7 convolution_convert_fusion.7
  268.3 2.1 fusion.63
  270.4 3.7 fusion.60
  274.1 6.2 %fusion = f32[8,128,512]{2,1,0:T(8,128)} fusion(f32[512,512]{1,0:T(8,128)} %subtract_maximum_fusion, f32[8]{0:T(128)} %copy-done.52, pred[512,512]{1,0:T(8,128)(4,1)S(1)} %copy-done.38, bf16[512,8,128]{0,2,1:T(8,128)(2,1)} %bitcast.169, bf16[512,8,128]{0,2,1:T(8,128)(2,1)S(1)} %bitcast.152, bf16[64,8,8,128]{3,2,1,0:T(8,128)(2,1)} %copy-done.21), kind=kOutput, calls=%fused_computation.10 | convolution fusion | flops 1082130432 | bytes 6553632 | tf_op jit(solution)/shard_map/hij,ihe->jhe/dot_general | solution.py:1267
  280.2 7.9 %convolution_convert_fusion.2 = bf16[2816,1024]{1,0:T(8,128)(2,1)} fusion(bf16[512,2816]{0,1:T(8,128)(2,1)} %bitcast.175, bf16[4,512,1024]{2,1,0:T(8,128)(2,1)} %param.23, s32[]{:T(128)S(6)} %select_n.19), kind=kOutput, calls=%fused_computation.9 | convolution fusion | flops 2955673600 | bytes 9699332 | tf_op jit(solution)/shard_map/dot_general | solution.py:33
  288.2 5.1 convolution_convert_fusion
  293.2 5.1 convolution_convert_fusion.1
  298.4 2.2 fusion.1
  300.7 1.8 fusion.28
  303.8 2.6 convolution_convert_fusion.4
  306.4 1.3 fusion.66
  311.1 1.3 fusion.65
  314.0 1.3 fusion.64
  316.4 1.6 fusion.10
  318.4 2.6 convolution_convert_fusion.5
  321.3 2.6 convolution_convert_fusion.6
  323.9 1.6 fusion.14.refs_9_
  325.5 256.0 %reduce_gradients.1 = (f32[704,128]{1,0:T(8,128)}, f32[704,128]{1,0:T(8,128)}, f32[704,128]{1,0:T(8,128)}, f32[256,128]{1,0:T(8,128)}, f32[256,128]{1,0:T(8,128)...) custom-call(bf16[4,704,1024]{2,1,0:T(8,128)(2,1)} %bitcast.162, ...), custom_call_target="tpu_custom_call" | custom-call | tf_op jit(solution)/shard_map/reduce_gradients/pallas_call | solution.py:808
  581.6 6.7 %convert_element_type.332 = f32[4,512,1024]{2,1,0:T(8,128)} convert(bf16[4,512,1024]{2,1,0:T(8,128)(2,1)} %get-tuple-element.59) | non-fusion elementwise | flops 2097152 | bytes 12582912 | tf_op jit(solution)/shard_map/convert_element_type | solution.py:1306
  591.3 4.7 copy.162
  (181 shorter events, 32.2 us)
Async XLA Ops:
  7.2 6.9 %copy-start.55 = (s32[4]{0:T(128)S(1)}, s32[4]{0:T(128)}, u32[]{:S(2)}) copy-start(s32[4]{0:T(128)} %refs_9_.1) | copy-start | bytes 52
  7.2 9.3 %copy-start.59 = (f32[2]{0:T(128)S(1)}, f32[2]{0:T(128)}, u32[]{:S(2)}) copy-start(f32[2]{0:T(128)} %param.21) | copy-start | bytes 28
  7.2 291.2 %all-gather.3.cloned.1.call-start = ((), (), s32[]{:S(2)}) async-start(), calls=%async_computation | async-start | bytes 2359296 | tf_op jit(solution)/shard_map/all_gather | solution.py:1226
  175.6 6.4 %copy-start.23 = (bf16[4,512,704]{2,1,0:T(8,128)(2,1)S(1)}, bf16[4,512,704]{2,1,0:T(8,128)(2,1)}, u32[]{:S(2)}) copy-start(bf16[4,512,704]{2,1,0:T(8,128)(2,1)} %get-tuple-element.43) | copy-start | bytes 8650756
  191.6 16.1 %slice-start.2 = ((s8[5767168]{0:T(1024)(128)(4,1)}), s8[1572864]{0:T(1024)(128)(4,1)S(1)}, s32[]{:S(2)}) async-start(s8[5767168]{0:T(1024)(128)(4,1)} %bitcast.194), calls=%async_computation.3 | async-start | bytes 3145728
  198.1 9.7 %slice-start.3 = ((s8[5767168]{0:T(1024)(128)(4,1)}), s8[4194304]{0:T(1024)(128)(4,1)S(1)}, s32[]{:S(2)}) async-start(s8[5767168]{0:T(1024)(128)(4,1)} %bitcast.194), calls=%async_computation.4 | async-start | bytes 8388608
  207.7 3.2 copy-start.24
  207.7 3.2 copy-start.26
  207.7 3.2 copy-start.31
  210.9 5.5 copy-start.39
  210.9 5.7 copy-start.20
  218.7 2.2 copy-start.29
  220.6 3.0 copy-start.1
  220.9 2.7 copy-start.37
  224.7 10.9 %copy-start.52 = (f32[8]{0:T(128)}, f32[8]{0:T(128)S(1)}, u32[]{:S(2)}) copy-start(f32[8]{0:T(128)S(1)} %neg.27) | copy-start | bytes 100
  230.7 4.8 copy-start.46
  231.6 7.0 %copy-start.19 = (bf16[512,4,256]{2,0,1:T(8,128)(2,1)S(1)}, bf16[512,4,256]{2,0,1:T(8,128)(2,1)}, u32[]{:S(2)}) copy-start(bf16[512,4,256]{2,0,1:T(8,128)(2,1)} %get-tuple-element.119) | copy-start | bytes 3145732
  233.4 6.6 %copy-start.18 = (bf16[512,4,256]{2,0,1:T(8,128)(2,1)S(1)}, bf16[512,4,256]{2,0,1:T(8,128)(2,1)}, u32[]{:S(2)}) copy-start(bf16[512,4,256]{2,0,1:T(8,128)(2,1)} %get-tuple-element.121) | copy-start | bytes 3145732
  248.9 4.8 copy-start.38
  259.2 2.2 copy-start.6
  259.2 2.6 copy-start.10
  259.3 2.9 copy-start.56
  262.2 2.7 copy-start.51
  262.2 2.7 copy-start.53
  262.2 2.7 copy-start.54
  262.2 3.4 copy-start.2
  262.2 3.4 copy-start.58
  265.6 4.8 slice-start
  265.6 2.7 copy-start.17
  265.6 4.8 slice-start.1
  280.2 7.9 %copy-start.27 = (bf16[512,2816]{1,0:T(8,128)(2,1)S(1)}, bf16[512,2816]{1,0:T(8,128)(2,1)}, u32[]{:S(2)}) copy-start(bf16[512,2816]{1,0:T(8,128)(2,1)} %copy-done.26) | copy-start | bytes 8650756
  280.2 7.9 %copy-start.32 = (bf16[512,1024]{1,0:T(8,128)(2,1)S(1)}, bf16[512,1024]{1,0:T(8,128)(2,1)}, u32[]{:S(2)}) copy-start(bf16[512,1024]{1,0:T(8,128)(2,1)} %get-tuple-element.42) | copy-start | bytes 3145732
  288.2 5.1 copy-start.25
  293.2 5.2 copy-start.49
  298.4 2.3 copy-start.8
  303.8 2.6 copy-start.14
  312.4 2.9 copy-start.15
  314.0 2.4 copy-start.11
  314.0 2.4 copy-start.48
  321.3 2.6 copy-start.3
  581.5 6.7 %copy-start.45 = (f32[256,128]{1,0:T(8,128)S(1)}, f32[256,128]{1,0:T(8,128)}, u32[]{:S(2)}) copy-start(f32[256,128]{1,0:T(8,128)} %get-tuple-element.60) | copy-start | bytes 393220
  581.5 7.5 %copy-start.44 = (f32[256,128]{1,0:T(8,128)S(1)}, f32[256,128]{1,0:T(8,128)}, u32[]{:S(2)}) copy-start(f32[256,128]{1,0:T(8,128)} %get-tuple-element.61) | copy-start | bytes 393220
  581.5 8.2 %copy-start.43 = (f32[256,128]{1,0:T(8,128)S(1)}, f32[256,128]{1,0:T(8,128)}, u32[]{:S(2)}) copy-start(f32[256,128]{1,0:T(8,128)} %get-tuple-element.62) | copy-start | bytes 393220
  581.6 9.0 %copy-start.42 = (f32[256,128]{1,0:T(8,128)S(1)}, f32[256,128]{1,0:T(8,128)}, u32[]{:S(2)}) copy-start(f32[256,128]{1,0:T(8,128)} %get-tuple-element.63) | copy-start | bytes 393220
  591.3 4.8 copy-start.41
  591.3 5.4 copy-start.36
  591.3 6.1 %copy-start.35 = (f32[704,128]{1,0:T(8,128)S(1)}, f32[704,128]{1,0:T(8,128)}, u32[]{:S(2)}) copy-start(f32[704,128]{1,0:T(8,128)} %get-tuple-element.66) | copy-start | bytes 1081348
  591.3 6.9 %copy-start.34 = (f32[704,128]{1,0:T(8,128)S(1)}, f32[704,128]{1,0:T(8,128)}, u32[]{:S(2)}) copy-start(f32[704,128]{1,0:T(8,128)} %get-tuple-element.170) | copy-start | bytes 1081348
  (17 other events, 26.8 us)
Sparse Core Ops, SparseCore 0:
  233.5 26.1 all-gather.2
